TPU v7x, 32 devices: a whole 2x2x4 slice. The times are simulated.
32 devices in a mesh: gx: 8 (over z, core), gy: 4 (over y, x).
Axes of the slice: x: 2, y: 2, z: 4, core: 2. Of those that a mesh axis runs over, the one named last changes fastest.
Arguments:
- design: float32 [64, 32, 128], P('gx', 'gy'), may hold values from 0.06 to 0.9
- passive: int32 [64, 32, 128], P('gx', 'gy'), may hold values 0 or 1
- basis_pairs: float32 [4, 2, 3, 64, 32, 128], P(None, None, None, 'gx', 'gy'), may hold values from -6 to 6
- supports: int32 [64, 32, 128], P('gx', 'gy'), may hold values 0 or 1
- stiffness: float32 [24, 24], replicated, may hold values from -1.25 to 1.25
- mass_matrix: float32 [24, 24], replicated, may hold values from -1.25 to 1.25
- volume_fraction: float32 [64], replicated, may hold values from 0.26 to 0.36
Outputs:
- sensitivity: float32 [64, 32, 128], P('gx', 'gy')
- design_next: float32 [64, 32, 128], P('gx', 'gy')
All inputs are finite; a program needn't handle non-finite values. No bound on the sum of `passive` or of `supports` on one device may be relied on, other than what follows from the above.
Results may differ from a plain program's by a relative error of at most 0.0003.
Values sent between devices are 32-bit elements; how exact they have to be, the bound alone decides.
A program may use at most 64 MiB of HBM per device.

v0:
```python
import math

import jax
import jax.numpy as jnp
from jax import lax
from jax.sharding import PartitionSpec as P

BISECT = 6
REGIONS = 64


PENALTY_SCALE = 3.0 * (1.0 - 0.001)
OMEGA_SQUARED = 0.5
MOVE_LIMIT = 0.2


def with_halo(cells, sides, width):
    for axis, dim in sides:
        count = lax.axis_size(axis)
        ends = count - 1
        head = lax.slice_in_dim(cells, 0, width, axis=dim)
        tail = lax.slice_in_dim(cells, cells.shape[dim] - width, cells.shape[dim], axis=dim)
        cells = jnp.concatenate(
            [
                lax.ppermute(tail, axis, [(i, (i + 1) % count) for i in range(ends)]),
                cells,
                lax.ppermute(head, axis, [((i + 1) % count, i) for i in range(ends)]),
            ],
            axis=dim,
        )
    return cells


def from_behind(value, axis, steps):
    count = lax.axis_size(axis)
    initial, last = (max(0, -steps), min(count, count - steps))
    return lax.ppermute(value, axis, [(source, source + steps) for source in range(initial, last)])


def filter_taps():
    tap_list = []
    for offset_x in range(-2, 3):
        for offset_y in range(-2, 3):
            for offset_z in range(-2, 3):
                weight = 3.0 - math.sqrt(
                    offset_x * offset_x + offset_y * offset_y + offset_z * offset_z
                )
                if weight > 0.0:
                    tap_list.append((offset_x, offset_y, offset_z, weight))
    return tap_list


def stencil(padded, block_shape):
    result = jnp.zeros(block_shape, jnp.float32)
    for offset_x, offset_y, offset_z, weight in filter_taps():
        result = (
            result
            + weight
            * padded[
                2 + offset_x : 2 + offset_x + block_shape[0],
                2 + offset_y : 2 + offset_y + block_shape[1],
                2 + offset_z : 2 + offset_z + block_shape[2],
            ]
        )
    return result


def element_terms(extended, stiffness, mass_matrix):
    pair_count = extended.shape[0]
    cells_x = extended.shape[3] - 1
    cells_y = extended.shape[4] - 1
    cells_z = extended.shape[5] - 1
    stiff_energy = jnp.zeros((cells_x * cells_y * cells_z,), jnp.float32)
    mass_energy = jnp.zeros((cells_x * cells_y * cells_z,), jnp.float32)
    for pair_index in range(pair_count):
        vectors = []
        for member in range(2):
            row_list = []
            for corner_x in (0, 1):
                for corner_y in (0, 1):
                    for corner_z in (0, 1):
                        for component in range(3):
                            row_list.append(
                                extended[
                                    pair_index,
                                    member,
                                    component,
                                    corner_x : corner_x + cells_x,
                                    corner_y : corner_y + cells_y,
                                    corner_z : corner_z + cells_z,
                                ].reshape(-1)
                            )
            vectors.append(jnp.stack(row_list))
        state_rows, adjoint_rows = vectors
        stiff_energy = stiff_energy + jnp.sum(
            state_rows * jnp.dot(stiffness, adjoint_rows, precision=lax.Precision.HIGHEST), axis=0
        )
        mass_energy = mass_energy + jnp.sum(
            state_rows * jnp.dot(mass_matrix, adjoint_rows, precision=lax.Precision.HIGHEST), axis=0
        )
    return (
        stiff_energy.reshape(cells_x, cells_y, cells_z),
        mass_energy.reshape(cells_x, cells_y, cells_z),
    )


def shards(design, passive, basis_pairs, supports, stiffness, mass_matrix, volume_fraction):
    block_shape = design.shape
    size_x, size_y, size_z = block_shape
    devices_x = lax.axis_size("gx")
    devices_y = lax.axis_size("gy")
    index_x = lax.axis_index("gx")
    index_y = lax.axis_index("gy")
    grid_x = size_x * devices_x
    grid_y = size_y * devices_y
    spread_x = jnp.arange(size_x + 4, dtype=jnp.int32) + index_x * size_x - 2
    spread_y = jnp.arange(size_y + 4, dtype=jnp.int32) + index_y * size_y - 2
    valid_x = ((spread_x >= 0) & (spread_x < grid_x)).astype(jnp.float32)
    valid_y = ((spread_y >= 0) & (spread_y < grid_y)).astype(jnp.float32)
    valid_z = jnp.pad(jnp.ones((size_z,), jnp.float32), 2)
    inside = valid_x[:, None, None] * valid_y[None, :, None] * valid_z[None, None, :]
    weight_sum = stencil(inside, block_shape)
    design_wide = with_halo(design, (("gx", 0), ("gy", 1)), 2)
    design_wide = jnp.pad(design_wide, ((0, 0), (0, 0), (2, 2)))
    physical = jnp.where(passive == 1, 1.0, stencil(design_wide, block_shape) / weight_sum)
    fields = basis_pairs * (1 - supports).astype(jnp.float32)
    rim_first = from_behind(fields[:, :, :, :1], "gx", -1)
    widened = jnp.concatenate([fields, rim_first], axis=3)
    rim_second = from_behind(widened[:, :, :, :, :1], "gy", -1)
    extended = jnp.concatenate([widened, rim_second], axis=4)
    extended = jnp.pad(extended, ((0, 0), (0, 0), (0, 0), (0, 0), (0, 0), (0, 1)))
    stiff_energy, mass_energy = element_terms(extended, stiffness, mass_matrix)
    raw_sensitivity = -(
        PENALTY_SCALE * physical * physical * stiff_energy - OMEGA_SQUARED * mass_energy
    )
    raw_sensitivity = jnp.where(passive == 1, 0.0, raw_sensitivity)
    scaled_wide = with_halo(raw_sensitivity / weight_sum, (("gx", 0), ("gy", 1)), 2)
    scaled_wide = jnp.pad(scaled_wide, ((0, 0), (0, 0), (2, 2)))
    sensitivity = stencil(scaled_wide, block_shape)
    benefit = jnp.maximum(-sensitivity, 0.0)
    floor_value = jnp.maximum(design - MOVE_LIMIT, 0.0)
    ceiling = jnp.minimum(design + MOVE_LIMIT, 1.0)
    band_cells = size_z // REGIONS
    target = volume_fraction * float(grid_x * grid_y * band_cells)

    def candidate(multiplier):
        per_cell = jnp.repeat(multiplier, band_cells)[None, None, :]
        trial = design * jnp.sqrt(benefit / per_cell)
        return jnp.where(passive == 1, 1.0, jnp.minimum(ceiling, jnp.maximum(floor_value, trial)))

    def region_sum(field):
        return jnp.sum(field, axis=(0, 1)).reshape(REGIONS, band_cells).sum(axis=1)

    levels = 1

    def bisect_round(round_index, bracket):
        low_end, high_end = bracket
        level_nodes = [(low_end, high_end)]
        midpoints = []
        next_nodes = []
        for node_low, node_high in level_nodes:
            middle = jnp.sqrt(node_low * node_high)
            midpoints.append(middle)
            next_nodes.append((node_low, middle))
            next_nodes.append((middle, node_high))
        partial_volumes = jnp.stack([region_sum(candidate(middle)) for middle in midpoints])
        volumes = lax.psum(partial_volumes, ("gx", "gy"))
        position = jnp.zeros((REGIONS,), jnp.int32)
        middle = jnp.sqrt(low_end * high_end)
        heap_index = position + (2**0 - 1)
        chosen = jnp.take_along_axis(volumes, heap_index[None, :], axis=0)[0]
        heavier = chosen > target
        low_end = jnp.where(heavier, middle, low_end)
        high_end = jnp.where(heavier, high_end, middle)
        return (low_end, high_end)

    start = (jnp.full((REGIONS,), 0.0001, jnp.float32), jnp.full((REGIONS,), 10000.0, jnp.float32))
    low_end, high_end = lax.fori_loop(0, BISECT // levels, bisect_round, start)
    design_next = candidate(jnp.sqrt(low_end * high_end))
    return (sensitivity, design_next)


def solution(mesh):
    placed = (
        P("gx", "gy", None),
        P("gx", "gy", None),
        P(None, None, None, "gx", "gy", None),
        P("gx", "gy", None),
        P(),
        P(),
        P(),
    )
    return jax.shard_map(
        shards,
        mesh=mesh,
        in_specs=placed,
        out_specs=(P("gx", "gy", None), P("gx", "gy", None)),
        check_vma=False,
    )
```

profile of v0, /device:TPU:0, one launch (start us, length us, event | category | flops | bytes accessed | tf_op | source)
XLA Modules:
  0.0 353.2 jit_solution(982225912130014539)
XLA Ops:
  2.7 3.0 collective-permute-start
  7.7 1.3 collective-permute-start.4
  10.0 4.8 %collective-permute-start.2 = (f32[12,2,128]{2,1,0:T(2,128)S(1)}, f32[12,2,128]{2,1,0:T(2,128)S(1)}, u32[]{:S(2)}, u32[]{:S(2)}) collective-permute-start(f32[12,2,128]{2,1,0:T(2,128)S(1)} %get-tuple-element.302), channel_id=1, source_target_pairs={{0,1},{1,2},{2,3},{4,5},{5,6},{6,7},{8,9},{9,10},{10,11},{12,13},{... | collective-permute-start | bytes 36872 | tf_op jit(solution)/shard_map/ppermute | solution.py:25
  14.9 1.3 collective-permute-start.3
  16.3 4.2 %collective-permute-done.3 = f32[12,2,128]{2,1,0:T(2,128)S(1)} collective-permute-done((f32[12,2,128]{2,1,0:T(2,128)S(1)}, f32[12,2,128]{2,1,0:T(2,128)S(1)}, u32[]{:S(2)}, u32[]{:S(2)}) %collective-permute-start.3) | collective-permute-done | bytes 12320 | tf_op jit(solution)/shard_map/ppermute | solution.py:27
  21.2 1.3 collective-permute-start.5
  24.7 6.2 %collective-permute-done.5 = f32[4,2,3,9,1,128]{5,3,4,2,1,0:T(8,128)S(1)} collective-permute-done((f32[4,2,3,9,1,128]{5,3,4,2,1,0:T(8,128)S(1)}, f32[4,2,3,9,1,128]{5,3,4,2,1,0:T(8,128)S(1)}, u32[]{:S(2)}, u32[]{:S(2)}) %collective-permute-start.5) | collective-permute-done | bytes 110624 | tf_op jit(solution)/shard_map/ppermute | solution.py:37
  37.0 3.7 %stack.27 = f32[24,8192]{1,0:T(8,128)S(1)} concatenate(f32[1,8192]{1,0:T(1,128)} %bitcast.406, f32[1,8192]{1,0:T(1,128)} %bitcast.405, f32[1,8192]{1,0:T(1,128)} %bitcast.404, f32[1,8192]{1,0:T(1,128)} %bitcast.454, f32[1,8192]{1,0:T(1,128)} %bitcast.327, f32[1,8192]{1,0:T(1,128)} %bitcast.328, f32[1,8192]{1,0:T(1,128)} %bitcast.453, f32[1,8192]{1,0:T(1,128)} %bitcast.452, ...), dimensions={0} | concatenate | bytes 1572864 | tf_op jit(solution)/shard_map/stack | solution.py:93
  40.7 5.8 %stack.28 = f32[24,8192]{1,0:T(8,128)} concatenate(f32[1,8192]{1,0:T(1,128)} %bitcast.401, f32[1,8192]{1,0:T(1,128)} %bitcast.400, f32[1,8192]{1,0:T(1,128)} %bitcast.418, f32[1,8192]{1,0:T(1,128)} %bitcast.298, f32[1,8192]{1,0:T(1,128)} %bitcast.299, f32[1,8192]{1,0:T(1,128)} %bitcast.300, f32[1,8192]{1,0:T(1,128)} %bitcast.447, f32[1,8192]{1,0:T(1,128)} %bitcast.446, ...), dimensions={0} | concatenate | bytes 1572864 | tf_op jit(solution)/shard_map/stack | solution.py:93
  46.5 2.7 fusion.12
  49.2 1.5 fusion.8
  50.7 3.7 %stack.34 = f32[24,8192]{1,0:T(8,128)S(1)} concatenate(f32[1,8192]{1,0:T(1,128)} %bitcast.394, f32[1,8192]{1,0:T(1,128)} %bitcast.414, f32[1,8192]{1,0:T(1,128)} %bitcast.410, f32[1,8192]{1,0:T(1,128)} %bitcast.344, f32[1,8192]{1,0:T(1,128)} %bitcast.345, f32[1,8192]{1,0:T(1,128)} %bitcast.346, f32[1,8192]{1,0:T(1,128)} %bitcast.361, f32[1,8192]{1,0:T(1,128)} %bitcast.360, ...), dimensions={0} | concatenate | bytes 1572864 | tf_op jit(solution)/shard_map/stack | solution.py:93
  54.4 5.8 %stack.33 = f32[24,8192]{1,0:T(8,128)} concatenate(f32[1,8192]{1,0:T(1,128)} %bitcast.388, f32[1,8192]{1,0:T(1,128)} %bitcast.387, f32[1,8192]{1,0:T(1,128)} %bitcast.386, f32[1,8192]{1,0:T(1,128)} %bitcast.296, f32[1,8192]{1,0:T(1,128)} %bitcast.309, f32[1,8192]{1,0:T(1,128)} %bitcast.310, f32[1,8192]{1,0:T(1,128)} %bitcast.343, f32[1,8192]{1,0:T(1,128)} %bitcast.342, ...), dimensions={0} | concatenate | bytes 1572864 | tf_op jit(solution)/shard_map/stack | solution.py:93
  60.2 2.7 fusion.15
  62.9 1.5 fusion.11
  66.3 3.6 %stack.30 = f32[24,8192]{1,0:T(8,128)S(1)} concatenate(f32[1,8192]{1,0:T(1,128)} %bitcast.399, f32[1,8192]{1,0:T(1,128)} %bitcast.398, f32[1,8192]{1,0:T(1,128)} %bitcast.397, f32[1,8192]{1,0:T(1,128)} %bitcast.364, f32[1,8192]{1,0:T(1,128)} %bitcast.365, f32[1,8192]{1,0:T(1,128)} %bitcast.366, f32[1,8192]{1,0:T(1,128)} %bitcast.440, f32[1,8192]{1,0:T(1,128)} %bitcast.439, ...), dimensions={0} | concatenate | bytes 1572864 | tf_op jit(solution)/shard_map/stack | solution.py:93
  70.2 3.6 %stack.29 = f32[24,8192]{1,0:T(8,128)S(1)} concatenate(f32[1,8192]{1,0:T(1,128)S(1)} %bitcast.393, f32[1,8192]{1,0:T(1,128)S(1)} %bitcast.392, f32[1,8192]{1,0:T(1,128)S(1)} %bitcast.391, f32[1,8192]{1,0:T(1,128)S(1)} %bitcast.280, f32[1,8192]{1,0:T(1,128)S(1)} %bitcast.281, f32[1,8192]{1,0:T(1,128)S(1)} %bitcast.282, f32[1,8192]{1,0:T(1,128)} %bitcast.441, f32[1,8192]{1,0:T(1,128)} %bitcast.437, ...), dimensions={0} | concatenate | bytes 1572864 | tf_op jit(solution)/shard_map/stack | solution.py:93
  75.8 3.4 stack.32
  79.3 3.4 stack.31
  85.9 1.7 collective-permute-start.6
  87.6 1.3 collective-permute-start.7
  88.9 3.2 collective-permute-done.7
  92.1 4.8 %collective-permute-start.8 = (f32[12,2,128]{2,1,0:T(2,128)S(1)}, f32[12,2,128]{2,1,0:T(2,128)S(1)}, u32[]{:S(2)}, u32[]{:S(2)}) collective-permute-start(f32[12,2,128]{2,1,0:T(2,128)S(1)} %get-tuple-element.300), channel_id=1, source_target_pairs={{0,1},{1,2},{2,3},{4,5},{5,6},{6,7},{8,9},{9,10},{10,11},{12,13},{... | collective-permute-start | bytes 36872 | tf_op jit(solution)/shard_map/ppermute | solution.py:25
  96.9 1.3 collective-permute-start.9
  98.3 4.2 %collective-permute-done.9 = f32[12,2,128]{2,1,0:T(2,128)S(1)} collective-permute-done((f32[12,2,128]{2,1,0:T(2,128)S(1)}, f32[12,2,128]{2,1,0:T(2,128)S(1)}, u32[]{:S(2)}, u32[]{:S(2)}) %collective-permute-start.9) | collective-permute-done | bytes 12320 | tf_op jit(solution)/shard_map/ppermute | solution.py:27
  103.3 249.0 %while.13 = (s32[]{:T(128)}, f32[64]{0:T(128)S(1)}, f32[64]{0:T(128)S(1)}, s32[8,8,128]{2,1,0:T(8,128)S(1)}, f32[8,8,128]{2,1,0:T(8,128)S(1)}, /*index=5*/f32[8,...) while((s32[]{:T(128)}, f32[64]{0:T(128)S(1)}, ...), condition=%wide.region_12.13_spmd.clone, body=%wide.region_8.12_spmd.clone.sunk | while | flops 57923 | bytes 172676 | solution.py:178
  103.9 40.3 %psum.9 = f32[1,64]{1,0:T(1,128)S(1)} all-reduce(f32[1,64]{1,0:T(1,128)S(1)} %bitcast.455), channel_id=1, replica_groups=mesh['gx'=8,'gy'=4] {'gx','gy'}, use_global_device_ids=true, to_apply=%region_11.11 | all-reduce | flops 64 | bytes 512 | tf_op jit(solution)/shard_map/while/body/eval_jaxpr/psum | solution.py:167
  145.5 40.4 %psum.9 = f32[1,64]{1,0:T(1,128)S(1)} all-reduce(f32[1,64]{1,0:T(1,128)S(1)} %bitcast.455), channel_id=1, replica_groups=mesh['gx'=8,'gy'=4] {'gx','gy'}, use_global_device_ids=true, to_apply=%region_11.11 | all-reduce | flops 64 | bytes 512 | tf_op jit(solution)/shard_map/while/body/eval_jaxpr/psum | solution.py:167
  187.3 39.7 %psum.9 = f32[1,64]{1,0:T(1,128)S(1)} all-reduce(f32[1,64]{1,0:T(1,128)S(1)} %bitcast.455), channel_id=1, replica_groups=mesh['gx'=8,'gy'=4] {'gx','gy'}, use_global_device_ids=true, to_apply=%region_11.11 | all-reduce | flops 64 | bytes 512 | tf_op jit(solution)/shard_map/while/body/eval_jaxpr/psum | solution.py:167
  228.4 40.4 %psum.9 = f32[1,64]{1,0:T(1,128)S(1)} all-reduce(f32[1,64]{1,0:T(1,128)S(1)} %bitcast.455), channel_id=1, replica_groups=mesh['gx'=8,'gy'=4] {'gx','gy'}, use_global_device_ids=true, to_apply=%region_11.11 | all-reduce | flops 64 | bytes 512 | tf_op jit(solution)/shard_map/while/body/eval_jaxpr/psum | solution.py:167
  270.1 39.7 %psum.9 = f32[1,64]{1,0:T(1,128)S(1)} all-reduce(f32[1,64]{1,0:T(1,128)S(1)} %bitcast.455), channel_id=1, replica_groups=mesh['gx'=8,'gy'=4] {'gx','gy'}, use_global_device_ids=true, to_apply=%region_11.11 | all-reduce | flops 64 | bytes 512 | tf_op jit(solution)/shard_map/while/body/eval_jaxpr/psum | solution.py:167
  311.2 40.4 %psum.9 = f32[1,64]{1,0:T(1,128)S(1)} all-reduce(f32[1,64]{1,0:T(1,128)S(1)} %bitcast.455), channel_id=1, replica_groups=mesh['gx'=8,'gy'=4] {'gx','gy'}, use_global_device_ids=true, to_apply=%region_11.11 | all-reduce | flops 64 | bytes 512 | tf_op jit(solution)/shard_map/while/body/eval_jaxpr/psum | solution.py:167
  (224 shorter events, 30.2 us)
Async XLA Ops:
  0.6 45.9 %copy-start = (f32[24,24]{1,0:T(8,128)S(1)}, f32[24,24]{1,0:T(8,128)}, u32[]{:S(2)}) copy-start(f32[24,24]{1,0:T(8,128)} %param.14) | copy-start | bytes 6916
  0.6 9.3 %copy-start.3 = (f32[8,8,128]{2,1,0:T(8,128)S(1)}, f32[8,8,128]{2,1,0:T(8,128)}, u32[]{:S(2)}) copy-start(f32[8,8,128]{2,1,0:T(8,128)} %param.9) | copy-start | bytes 98308
  1.4 8.6 %collective-permute-start.1 = (f32[2,8,128]{2,1,0:T(8,128)S(1)}, f32[2,8,128]{2,1,0:T(8,128)S(1)}, u32[]{:S(2)}, u32[]{:S(2)}) collective-permute-start(f32[2,8,128]{2,1,0:T(8,128)S(1)} %get-tuple-element.311), channel_id=1, source_target_pairs={{4,0},{8,4},{12,8},{16,12},{20,16},{24,20},{28,24},{5,1},{9,5},{13... | collective-permute-start | bytes 24584 | tf_op jit(solution)/shard_map/ppermute | solution.py:27
  2.7 7.3 %collective-permute-start = (f32[2,8,128]{2,1,0:T(8,128)S(1)}, f32[2,8,128]{2,1,0:T(8,128)S(1)}, u32[]{:S(2)}, u32[]{:S(2)}) collective-permute-start(f32[2,8,128]{2,1,0:T(8,128)S(1)} %get-tuple-element.312), channel_id=1, source_target_pairs={{0,4},{4,8},{8,12},{12,16},{16,20},{20,24},{24,28},{1,5},{5,9},{9,... | collective-permute-start | bytes 24584 | tf_op jit(solution)/shard_map/ppermute | solution.py:25
  7.7 12.9 %collective-permute-start.4 = (f32[4,2,3,1,8,128]{5,4,3,2,1,0:T(8,128)S(1)}, f32[4,2,3,1,8,128]{5,4,3,2,1,0:T(8,128)S(1)}, u32[]{:S(2)}, u32[]{:S(2)}) collective-permute-start(f32[4,2,3,1,8,128]{5,4,3,2,1,0:T(8,128)S(1)} %slice.2402), channel_id=1, source_target_pairs={{4,0},{8,4},{12,8},{16,12},{20,16},{24,20},{28,24},{5,1},{9,5},{13... | collective-permute-start | bytes 294920 | tf_op jit(solution)/shard_map/ppermute | solution.py:37
  10.0 6.2 %collective-permute-start.2 = (f32[12,2,128]{2,1,0:T(2,128)S(1)}, f32[12,2,128]{2,1,0:T(2,128)S(1)}, u32[]{:S(2)}, u32[]{:S(2)}) collective-permute-start(f32[12,2,128]{2,1,0:T(2,128)S(1)} %get-tuple-element.302), channel_id=1, source_target_pairs={{0,1},{1,2},{2,3},{4,5},{5,6},{6,7},{8,9},{9,10},{10,11},{12,13},{... | collective-permute-start | bytes 36872 | tf_op jit(solution)/shard_map/ppermute | solution.py:25
  14.9 5.6 %collective-permute-start.3 = (f32[12,2,128]{2,1,0:T(2,128)S(1)}, f32[12,2,128]{2,1,0:T(2,128)S(1)}, u32[]{:S(2)}, u32[]{:S(2)}) collective-permute-start(f32[12,2,128]{2,1,0:T(2,128)S(1)} %get-tuple-element.303), channel_id=1, source_target_pairs={{1,0},{2,1},{3,2},{5,4},{6,5},{7,6},{9,8},{10,9},{11,10},{13,12},{... | collective-permute-start | bytes 36872 | tf_op jit(solution)/shard_map/ppermute | solution.py:27
  21.2 9.8 %collective-permute-start.5 = (f32[4,2,3,9,1,128]{5,3,4,2,1,0:T(8,128)S(1)}, f32[4,2,3,9,1,128]{5,3,4,2,1,0:T(8,128)S(1)}, u32[]{:S(2)}, u32[]{:S(2)}) collective-permute-start(f32[4,2,3,9,1,128]{5,3,4,2,1,0:T(8,128)S(1)} %copy.107), channel_id=1, source_target_pairs={{1,0},{2,1},{3,2},{5,4},{6,5},{7,6},{9,8},{10,9},{11,10},{13,12},{... | collective-permute-start | bytes 331784 | tf_op jit(solution)/shard_map/ppermute | solution.py:37
  40.7 8.5 %copy-start.5 = (f32[24,24]{1,0:T(8,128)S(1)}, f32[24,24]{1,0:T(8,128)}, u32[]{:S(2)}) copy-start(f32[24,24]{1,0:T(8,128)} %param.13) | copy-start | bytes 6916
  65.3 4.7 %copy-start.13 = (f32[1,1,1,8,8,128]{5,4,3,2,1,0:T(8,128)S(1)}, f32[1,1,1,8,8,128]{5,4,3,2,1,0:T(8,128)}, u32[]{:S(2)}) copy-start(f32[1,1,1,8,8,128]{5,4,3,2,1,0:T(8,128)} %get-tuple-element.114) | copy-start | bytes 98308
  65.3 4.8 %copy-start.14 = (f32[1,1,1,8,8,128]{5,4,3,2,1,0:T(8,128)S(1)}, f32[1,1,1,8,8,128]{5,4,3,2,1,0:T(8,128)}, u32[]{:S(2)}) copy-start(f32[1,1,1,8,8,128]{5,4,3,2,1,0:T(8,128)} %get-tuple-element.115) | copy-start | bytes 98308
  65.3 4.8 %copy-start.15 = (f32[1,1,1,8,8,128]{5,4,3,2,1,0:T(8,128)S(1)}, f32[1,1,1,8,8,128]{5,4,3,2,1,0:T(8,128)}, u32[]{:S(2)}) copy-start(f32[1,1,1,8,8,128]{5,4,3,2,1,0:T(8,128)} %get-tuple-element.116) | copy-start | bytes 98308
  65.3 4.8 %copy-start.16 = (f32[1,1,1,8,8,128]{5,4,3,2,1,0:T(8,128)S(1)}, f32[1,1,1,8,8,128]{5,4,3,2,1,0:T(8,128)}, u32[]{:S(2)}) copy-start(f32[1,1,1,8,8,128]{5,4,3,2,1,0:T(8,128)} %get-tuple-element.117) | copy-start | bytes 98308
  65.3 4.8 %copy-start.17 = (f32[1,1,1,8,8,128]{5,4,3,2,1,0:T(8,128)S(1)}, f32[1,1,1,8,8,128]{5,4,3,2,1,0:T(8,128)}, u32[]{:S(2)}) copy-start(f32[1,1,1,8,8,128]{5,4,3,2,1,0:T(8,128)} %get-tuple-element.118) | copy-start | bytes 98308
  65.3 4.8 %copy-start.18 = (f32[1,1,1,8,8,128]{5,4,3,2,1,0:T(8,128)S(1)}, f32[1,1,1,8,8,128]{5,4,3,2,1,0:T(8,128)}, u32[]{:S(2)}) copy-start(f32[1,1,1,8,8,128]{5,4,3,2,1,0:T(8,128)} %get-tuple-element.119) | copy-start | bytes 98308
  65.3 4.8 %copy-start.19 = (f32[1,1,1,8,8,128]{5,4,3,2,1,0:T(8,128)S(1)}, f32[1,1,1,8,8,128]{5,4,3,2,1,0:T(8,128)}, u32[]{:S(2)}) copy-start(f32[1,1,1,8,8,128]{5,4,3,2,1,0:T(8,128)} %get-tuple-element.120) | copy-start | bytes 98308
  65.3 4.8 %copy-start.20 = (f32[1,1,1,8,8,128]{5,4,3,2,1,0:T(8,128)S(1)}, f32[1,1,1,8,8,128]{5,4,3,2,1,0:T(8,128)}, u32[]{:S(2)}) copy-start(f32[1,1,1,8,8,128]{5,4,3,2,1,0:T(8,128)} %get-tuple-element.121) | copy-start | bytes 98308
  65.3 4.8 %copy-start.21 = (f32[1,1,1,8,8,128]{5,4,3,2,1,0:T(8,128)S(1)}, f32[1,1,1,8,8,128]{5,4,3,2,1,0:T(8,128)}, u32[]{:S(2)}) copy-start(f32[1,1,1,8,8,128]{5,4,3,2,1,0:T(8,128)} %get-tuple-element.122) | copy-start | bytes 98308
  65.3 4.8 %copy-start.22 = (f32[1,1,1,8,8,128]{5,4,3,2,1,0:T(8,128)S(1)}, f32[1,1,1,8,8,128]{5,4,3,2,1,0:T(8,128)}, u32[]{:S(2)}) copy-start(f32[1,1,1,8,8,128]{5,4,3,2,1,0:T(8,128)} %get-tuple-element.123) | copy-start | bytes 98308
  65.3 4.8 %copy-start.23 = (f32[1,1,1,8,8,128]{5,4,3,2,1,0:T(8,128)S(1)}, f32[1,1,1,8,8,128]{5,4,3,2,1,0:T(8,128)}, u32[]{:S(2)}) copy-start(f32[1,1,1,8,8,128]{5,4,3,2,1,0:T(8,128)} %get-tuple-element.124) | copy-start | bytes 98308
  74.8 4.5 %copy-start.34 = (f32[1,1,1,8,8,128]{5,4,3,2,1,0:T(8,128)S(1)}, f32[1,1,1,8,8,128]{5,4,3,2,1,0:T(8,128)}, u32[]{:S(2)}) copy-start(f32[1,1,1,8,8,128]{5,4,3,2,1,0:T(8,128)} %get-tuple-element.291) | copy-start | bytes 98308
  74.8 4.5 %copy-start.35 = (f32[1,1,1,8,8,128]{5,4,3,2,1,0:T(8,128)S(1)}, f32[1,1,1,8,8,128]{5,4,3,2,1,0:T(8,128)}, u32[]{:S(2)}) copy-start(f32[1,1,1,8,8,128]{5,4,3,2,1,0:T(8,128)} %get-tuple-element.292) | copy-start | bytes 98308
  74.8 4.5 %copy-start.36 = (f32[1,1,1,8,8,128]{5,4,3,2,1,0:T(8,128)S(1)}, f32[1,1,1,8,8,128]{5,4,3,2,1,0:T(8,128)}, u32[]{:S(2)}) copy-start(f32[1,1,1,8,8,128]{5,4,3,2,1,0:T(8,128)} %get-tuple-element.293) | copy-start | bytes 98308
  74.8 4.5 %copy-start.40 = (f32[1,1,1,8,8,128]{5,4,3,2,1,0:T(8,128)S(1)}, f32[1,1,1,8,8,128]{5,4,3,2,1,0:T(8,128)}, u32[]{:S(2)}) copy-start(f32[1,1,1,8,8,128]{5,4,3,2,1,0:T(8,128)} %get-tuple-element.262) | copy-start | bytes 98308
  74.8 4.5 %copy-start.41 = (f32[1,1,1,8,8,128]{5,4,3,2,1,0:T(8,128)S(1)}, f32[1,1,1,8,8,128]{5,4,3,2,1,0:T(8,128)}, u32[]{:S(2)}) copy-start(f32[1,1,1,8,8,128]{5,4,3,2,1,0:T(8,128)} %get-tuple-element.263) | copy-start | bytes 98308
  74.8 4.5 %copy-start.42 = (f32[1,1,1,8,8,128]{5,4,3,2,1,0:T(8,128)S(1)}, f32[1,1,1,8,8,128]{5,4,3,2,1,0:T(8,128)}, u32[]{:S(2)}) copy-start(f32[1,1,1,8,8,128]{5,4,3,2,1,0:T(8,128)} %get-tuple-element.264) | copy-start | bytes 98308
  84.6 13.6 %copy-start.57 = (f32[64]{0:T(128)S(1)}, f32[64]{0:T(128)}, u32[]{:S(2)}) copy-start(f32[64]{0:T(128)} %param.15) | copy-start | bytes 772
  85.9 3.0 collective-permute-start.6
  87.6 4.5 %collective-permute-start.7 = (f32[2,8,128]{2,1,0:T(8,128)S(1)}, f32[2,8,128]{2,1,0:T(8,128)S(1)}, u32[]{:S(2)}, u32[]{:S(2)}) collective-permute-start(f32[2,8,128]{2,1,0:T(8,128)S(1)} %get-tuple-element.310), channel_id=1, source_target_pairs={{4,0},{8,4},{12,8},{16,12},{20,16},{24,20},{28,24},{5,1},{9,5},{13... | collective-permute-start | bytes 24584 | tf_op jit(solution)/shard_map/ppermute | solution.py:27
  92.1 6.2 %collective-permute-start.8 = (f32[12,2,128]{2,1,0:T(2,128)S(1)}, f32[12,2,128]{2,1,0:T(2,128)S(1)}, u32[]{:S(2)}, u32[]{:S(2)}) collective-permute-start(f32[12,2,128]{2,1,0:T(2,128)S(1)} %get-tuple-element.300), channel_id=1, source_target_pairs={{0,1},{1,2},{2,3},{4,5},{5,6},{6,7},{8,9},{9,10},{10,11},{12,13},{... | collective-permute-start | bytes 36872 | tf_op jit(solution)/shard_map/ppermute | solution.py:25
  96.9 5.6 %collective-permute-start.9 = (f32[12,2,128]{2,1,0:T(2,128)S(1)}, f32[12,2,128]{2,1,0:T(2,128)S(1)}, u32[]{:S(2)}, u32[]{:S(2)}) collective-permute-start(f32[12,2,128]{2,1,0:T(2,128)S(1)} %get-tuple-element.301), channel_id=1, source_target_pairs={{1,0},{2,1},{3,2},{5,4},{6,5},{7,6},{9,8},{10,9},{11,10},{13,12},{... | collective-permute-start | bytes 36872 | tf_op jit(solution)/shard_map/ppermute | solution.py:27
  103.3 249.3 %copy-start.33 = (f32[8,8,128]{2,1,0:T(8,128)}, f32[8,8,128]{2,1,0:T(8,128)S(1)}, u32[]{:S(2)}) copy-start(f32[8,8,128]{2,1,0:T(8,128)S(1)} %get-tuple-element.101) | copy-start | bytes 98308
  (36 other events, 85.3 us)
where the time goes:
time: 356 us; the launch traced here: 353 us
  blocking collectives  241 us (68%)
  local copies, waits for them, and re-layouts  50.1 us (14%)
  starting transfers between devices  22.2 us (6%)
  waiting for transfers between devices  17.8 us (5%)
  matrix products  11.6 us (3%)
  other arithmetic  8.48 us (2%)
    psum x6, blocking collectives, bisect_round(): volumes = lax.psum(partial_volumes, ('gx', 'gy'))  241 us
    another operation x8, local copies, waits for them, and re-layouts, element_terms(): vectors.append(jnp.stack(row_list))  33.2 us
    ppermute x4, starting transfers between devices, with_halo(): lax.ppermute(tail, axis, [(i, (i + 1) % count) for i in range(ends)])  14.4 us
    ppermute x4, waiting for transfers between devices, with_halo(): lax.ppermute(head, axis, [((i + 1) % count, i) for i in range(ends)])  11.6 us
    slice x9, local copies, waits for them, and re-layouts, element_terms(): extended[pair_index, member, component, corner_x:corner_x + cells_x, corn...  8.39 us
  transfers between devices with their start and end apart: 10, of which 4 were waited for; matrix products, arithmetic and copies ran while one was open for 2% of the time, Pallas kernels for 0%

commit v1 on v0

v1 whole, which is shorter than its diff:
```python
import functools
import math

import jax
import jax.numpy as jnp
from jax import lax
from jax.experimental import pallas as pl
from jax.experimental.pallas import tpu as pltpu
from jax.sharding import PartitionSpec as P

PENALTY_SCALE = 3.0 * (1.0 - 0.001)
OMEGA_SQUARED = 0.5
MOVE_LIMIT = 0.2
LEVELS = 3
ROUNDS = 2
MESH = pl.DeviceIdType.MESH
AROUND = ((-1, 0), (1, 0), (0, -1), (0, 1), (-1, -1), (-1, 1), (1, -1), (1, 1))


def opposite(slot):
    dx, dy = AROUND[slot]
    return AROUND.index((-dx, -dy))


def z_shift(value, step):
    axis = value.ndim - 1
    size = value.shape[axis]
    lane = lax.broadcasted_iota(jnp.int32, value.shape, axis)
    moved = pltpu.roll(value, (-step) % size, axis)
    keep = lane < size - step if step > 0 else lane >= -step
    return jnp.where(keep, moved, 0.0)


def stencil(rows_at, size_x):
    spread = [[None] * (size_x + 4) for _ in range(3)]
    for plane in range(size_x + 4):
        tiles = [rows_at(plane, oy) for oy in range(-2, 3)]
        folded_y = (tiles[2], tiles[1] + tiles[3], tiles[0] + tiles[4])
        parts = [[], [], []]
        for cy, tile in enumerate(folded_y):
            folded_z = (
                tile,
                z_shift(tile, 1) + z_shift(tile, -1),
                z_shift(tile, 2) + z_shift(tile, -2),
            )
            for cz, entry in enumerate(folded_z):
                for cx in range(3):
                    weight = 3.0 - math.sqrt(cx * cx + cy * cy + cz * cz)
                    if weight > 0.0:
                        parts[cx].append(weight * entry)
        for cx in range(3):
            spread[cx][plane] = functools.reduce(lambda a, b: a + b, parts[cx])
    return [
        spread[0][i + 2]
        + (spread[1][i + 1] + spread[1][i + 3])
        + (spread[2][i] + spread[2][i + 4])
        for i in range(size_x)
    ]


def kernel(
    nx, ny, size_x, size_y, size_z, pairs, regions,
    design, passive, basis, supports, stiffness, mass_matrix, fraction,
    sensitivity, design_next,
    fields, send_x, send_y, send_c, recv_x, recv_y, recv_c,
    edge_send, edge_recv, wide, scaled, weights_hi, weights_lo, weight_sum, physical, energy,
    gather_y, gather_x,
    basis_send_sem, basis_recv_sem, halo_send_sem, halo_recv_sem,
    gy_send_sem, gy_recv_sem, gx_send_sem, gx_recv_sem,
):
    ix, iy = lax.axis_index("gx"), lax.axis_index("gy")
    pitch = 2 * size_y
    cells = size_x * size_y

    def there(dx, dy):
        return (
            (ix + dx >= 0) & (ix + dx < nx) & (iy + dy >= 0) & (iy + dy < ny)
        )

    barrier = pltpu.get_barrier_semaphore()
    for step in range(1, ny):
        pl.semaphore_signal(barrier, inc=1, device_id=(ix, lax.rem(iy + step, ny)), device_id_type=MESH)
    for step in range(1, nx):
        pl.semaphore_signal(barrier, inc=1, device_id=(lax.rem(ix + step, nx), iy), device_id_type=MESH)
    for dx, dy in AROUND[4:]:
        @pl.when(there(dx, dy))
        def _(dx=dx, dy=dy):
            pl.semaphore_signal(barrier, inc=1, device_id=(ix + dx, iy + dy), device_id_type=MESH)
    corners = sum(there(dx, dy).astype(jnp.int32) for dx, dy in AROUND[4:])

    free = 1.0 - supports[...].astype(jnp.float32)
    send_x[...] = basis[:, 0:size_y, :] * free[0:size_y][None]
    free_y = 1.0 - supports[pl.ds(0, size_x, stride=size_y), :].astype(jnp.float32)
    for f in range(6 * pairs):
        rows = basis[f, pl.ds(0, size_x, stride=size_y), :] * free_y
        send_y[f] = rows
        send_c[pl.ds(f, 1), :] = rows[0:1]

    def pack_edges(source, which):
        for x in range(2):
            edge_send[which, 2, x] = source[pl.ds(x * size_y, size_y), :]
            edge_send[which, 3, x] = source[pl.ds((size_x - 2 + x) * size_y, size_y), :]
        for y in range(2):
            edge_send[which, 0, y] = source[pl.ds(y, size_x, stride=size_y), :]
            edge_send[which, 1, y] = source[pl.ds(size_y - 2 + y, size_x, stride=size_y), :]

    def edge_copies(which):
        copies = []
        for slot, (dx, dy) in enumerate(AROUND):
            if dy == 0:
                src = edge_send.at[which, 2 if dx < 0 else 3]
            else:
                src = edge_send.at[which, 0 if dy < 0 else 1]
            copies.append(pltpu.make_async_remote_copy(
                src_ref=src,
                dst_ref=edge_recv.at[which, opposite(slot)],
                send_sem=halo_send_sem.at[which, slot],
                recv_sem=halo_recv_sem.at[which, opposite(slot)],
                device_id=(ix + dx, iy + dy),
                device_id_type=MESH,
            ))
        return copies

    def edge_start(copies):
        for (dx, dy), copy in zip(AROUND, copies):
            @pl.when(there(dx, dy))
            def _(copy=copy):
                copy.start()

    def edge_receive(copies, which):
        for slot, (dx, dy) in enumerate(AROUND):
            copy = copies[opposite(slot)]

            @pl.when(there(dx, dy))
            def _(copy=copy):
                copy.wait_recv()

            @pl.when(jnp.logical_not(there(dx, dy)))
            def _(slot=slot):
                edge_recv[which, slot] = jnp.zeros((2, size_y, size_z), jnp.float32)

    def edge_finish(copies):
        for (dx, dy), copy in zip(AROUND, copies):
            @pl.when(there(dx, dy))
            def _(copy=copy):
                copy.wait_send()

    span = 3 * size_y

    def assemble(source, which):
        for x in range(size_x):
            wide[pl.ds((x + 2) * span + size_y, size_y), :] = source[pl.ds(x * size_y, size_y), :]
        for x in range(2):
            wide[pl.ds(x * span + size_y, size_y), :] = edge_recv[which, 0, x]
            wide[pl.ds((size_x + 2 + x) * span + size_y, size_y), :] = edge_recv[which, 1, x]
        for y in range(2):
            low, high = size_y - 2 + y, 2 * size_y + y
            wide[pl.ds(2 * span + low, size_x, stride=span), :] = edge_recv[which, 2, y]
            wide[pl.ds(2 * span + high, size_x, stride=span), :] = edge_recv[which, 3, y]
            for x in range(2):
                for slot, row in ((4, low), (5, high)):
                    wide[pl.ds(x * span + row, 1), :] = edge_recv[which, slot, y, size_x - 2 + x : size_x - 1 + x, :]
                for slot, row in ((6, low), (7, high)):
                    wide[pl.ds((size_x + 2 + x) * span + row, 1), :] = edge_recv[which, slot, y, x : x + 1, :]

    def wide_rows(plane, oy):
        return wide[pl.ds(plane * span + size_y + oy, size_y), :]

    pack_edges(design, 0)

    pl.semaphore_wait(barrier, (nx - 1) + (ny - 1) + corners)

    design_copies = edge_copies(0)
    edge_start(design_copies)
    basis_steps = ((-1, 0), (0, -1), (-1, -1))
    basis_copies = [
        pltpu.make_async_remote_copy(
            src_ref=src, dst_ref=dst, send_sem=basis_send_sem.at[k], recv_sem=basis_recv_sem.at[k],
            device_id=(ix + dx, iy + dy), device_id_type=MESH,
        )
        for k, ((dx, dy), src, dst) in enumerate(
            zip(basis_steps, (send_x, send_y, send_c), (recv_x, recv_y, recv_c))
        )
    ]
    for (dx, dy), copy in zip(basis_steps, basis_copies):
        @pl.when(there(dx, dy))
        def _(copy=copy):
            copy.start()

    for x in range(size_x):
        fields[:, x * pitch : x * pitch + size_y, :] = (
            basis[:, x * size_y : (x + 1) * size_y, :] * free[x * size_y : (x + 1) * size_y][None]
        )

    wide_n, narrow_n = 24 * size_y, 24
    row = lax.broadcasted_iota(jnp.int32, (wide_n, narrow_n), 0)
    col = lax.broadcasted_iota(jnp.int32, (wide_n, narrow_n), 1)
    expand = (row // size_y == col).astype(jnp.float32).astype(jnp.bfloat16)
    row_t = lax.broadcasted_iota(jnp.int32, (narrow_n, wide_n), 0)
    col_t = lax.broadcasted_iota(jnp.int32, (narrow_n, wide_n), 1)
    expand_t = (col_t // size_y == row_t).astype(jnp.float32).astype(jnp.bfloat16)
    same = (
        lax.broadcasted_iota(jnp.int32, (wide_n, wide_n), 0) % size_y
        == lax.broadcasted_iota(jnp.int32, (wide_n, wide_n), 1) % size_y
    )

    def spread_matrix(piece):
        tall = jnp.dot(expand, piece, preferred_element_type=jnp.float32).astype(jnp.bfloat16)
        full = jnp.dot(tall, expand_t, preferred_element_type=jnp.float32)
        return jnp.where(same, full, 0.0).astype(jnp.bfloat16)

    for k, matrix in enumerate((stiffness, mass_matrix)):
        value = matrix[...]
        high = value.astype(jnp.bfloat16)
        low = (value - high.astype(jnp.float32)).astype(jnp.bfloat16)
        weights_hi[pl.ds(k * wide_n, wide_n), :] = spread_matrix(high)
        weights_lo[pl.ds(k * wide_n, wide_n), :] = spread_matrix(low)

    row_y = lax.broadcasted_iota(jnp.int32, (size_y, size_z), 0)
    grid_x, grid_y = nx * size_x, ny * size_y

    def inside(plane, oy):
        at_x = ix * size_x + plane - 2
        at_y = row_y + (iy * size_y + oy)
        ok = (at_y >= 0) & (at_y < grid_y) & (at_x >= 0) & (at_x < grid_x)
        return jnp.where(ok, 1.0, 0.0)

    for x, tile in enumerate(stencil(inside, size_x)):
        weight_sum[pl.ds(x * size_y, size_y), :] = tile

    edge_receive(design_copies, 0)
    assemble(design, 0)
    for x, tile in enumerate(stencil(wide_rows, size_x)):
        at = pl.ds(x * size_y, size_y)
        physical[at, :] = jnp.where(passive[at, :] == 1, 1.0, tile / weight_sum[at, :])

    for (dx, dy), copy, buffer in zip(basis_steps, basis_copies, (recv_x, recv_y, recv_c)):
        @pl.when(there(-dx, -dy))
        def _(copy=copy):
            copy.wait_recv()

        @pl.when(jnp.logical_not(there(-dx, -dy)))
        def _(buffer=buffer):
            buffer[...] = jnp.zeros(buffer.shape, jnp.float32)

    fields[:, size_x * pitch : size_x * pitch + size_y, :] = recv_x[...]
    for f in range(6 * pairs):
        fields[f, pl.ds(size_y, size_x, stride=pitch), :] = recv_y[f]
        fields[f, pl.ds(size_x * pitch + size_y, 1), :] = recv_c[pl.ds(f, 1), :]

    energy[...] = jnp.zeros((2 * cells, size_z), jnp.float32)

    def pair_step(pair, carry):
        def corner_tiles(member):
            tiles = {}
            for c in range(3):
                f = pair * 6 + member * 3 + c
                for x in range(size_x + 1):
                    for b in range(2):
                        tile = fields[f, x * pitch + b : x * pitch + b + size_y, :]
                        tiles[c, x, b, 0] = tile
                        tiles[c, x, b, 1] = z_shift(tile, 1)
            return tiles

        order = [(a, b, d, c) for a in range(2) for b in range(2) for d in range(2) for c in range(3)]
        adjoint = corner_tiles(1)
        operand = jnp.concatenate(
            [
                jnp.concatenate([adjoint[c, x + a, b, d] for x in range(size_x)], axis=1)
                for a, b, d, c in order
            ],
            axis=0,
        )
        high = operand.astype(jnp.bfloat16)
        low = (operand - high.astype(jnp.float32)).astype(jnp.bfloat16)
        product = (
            jnp.dot(weights_hi[...], high, preferred_element_type=jnp.float32)
            + jnp.dot(weights_hi[...], low, preferred_element_type=jnp.float32)
            + jnp.dot(weights_lo[...], high, preferred_element_type=jnp.float32)
        )
        state = corner_tiles(0)
        for x in range(size_x):
            for k in range(2):
                total = energy[pl.ds((k * size_x + x) * size_y, size_y), :]
                for r, (a, b, d, c) in enumerate(order):
                    at = k * wide_n + r * size_y
                    total = total + state[c, x + a, b, d] * product[at : at + size_y, x * size_z : (x + 1) * size_z]
                energy[pl.ds((k * size_x + x) * size_y, size_y), :] = total
        return carry

    lax.fori_loop(0, pairs, pair_step, 0)

    solid = passive[...] == 1
    density = physical[...]
    raw = -(
        PENALTY_SCALE * density * density * energy[0:cells, :]
        - OMEGA_SQUARED * energy[cells : 2 * cells, :]
    )
    scaled[...] = jnp.where(solid, 0.0, raw) / weight_sum[...]

    pack_edges(scaled, 1)
    scaled_copies = edge_copies(1)
    edge_start(scaled_copies)
    edge_receive(scaled_copies, 1)
    assemble(scaled, 1)
    for x, tile in enumerate(stencil(wide_rows, size_x)):
        sensitivity[pl.ds(x * size_y, size_y), :] = tile

    value = design[...]
    gain = value * jnp.sqrt(jnp.maximum(-sensitivity[...], 0.0))
    floor_value = jnp.maximum(value - MOVE_LIMIT, 0.0)
    ceiling = jnp.minimum(value + MOVE_LIMIT, 1.0)

    def candidate(multiplier):
        trial = gain * (1.0 / jnp.sqrt(multiplier))
        return jnp.where(solid, 1.0, jnp.minimum(ceiling, jnp.maximum(floor_value, trial)))

    band = size_z // regions
    pick = (
        lax.broadcasted_iota(jnp.int32, (regions, size_z), 1) // band
        == lax.broadcasted_iota(jnp.int32, (regions, size_z), 0)
    ).astype(jnp.float32).astype(jnp.bfloat16)
    rest = jnp.broadcast_to(fraction[...], (8, regions))
    target = jnp.zeros((8, size_z), jnp.float32)
    for _ in range(3):
        piece = rest.astype(jnp.bfloat16)
        target = target + jnp.dot(piece, pick, preferred_element_type=jnp.float32)
        rest = rest - piece.astype(jnp.float32)
    target = target[0:1] * float(grid_x * grid_y * band)

    lane = lax.broadcasted_iota(jnp.int32, (8, size_z), 1)
    slot_row = lax.broadcasted_iota(jnp.int32, (8, size_z), 0)
    low_end = jnp.full((1, size_z), 1e-4, jnp.float32)
    high_end = jnp.full((1, size_z), 1e4, jnp.float32)
    pending = []

    def line_sum(part, buffer, round_index, count, me, target_of, send_sem, recv_sem):
        buffer[round_index, pl.ds(me, 1)] = part[None]
        copies = []
        for step in range(1, count):
            copy = pltpu.make_async_remote_copy(
                src_ref=buffer.at[round_index, me],
                dst_ref=buffer.at[round_index, me],
                send_sem=send_sem.at[round_index, step],
                recv_sem=recv_sem.at[round_index, step],
                device_id=target_of(lax.rem(me + step, count)),
                device_id_type=MESH,
            )
            copy.start()
            copies.append(copy)
        for copy in copies:
            copy.wait_recv()
        pending.extend(copies)
        return functools.reduce(lambda a, b: a + b, [buffer[round_index, k] for k in range(count)])

    for round_index in range(ROUNDS):
        nodes = [(low_end, high_end)]
        middles = []
        for level in range(LEVELS):
            following = []
            for node_low, node_high in nodes:
                middle = jnp.sqrt(node_low * node_high)
                middles.append(middle)
                following += [(node_low, middle), (middle, node_high)]
            nodes = following
        volumes = jnp.zeros((8, size_z), jnp.float32)
        for k, middle in enumerate(middles):
            trial = candidate(middle).reshape(size_x, size_y, size_z)
            column = jnp.sum(jnp.sum(trial, axis=0), axis=0, keepdims=True)
            volumes = jnp.where(slot_row == k, column, volumes)
        volumes = line_sum(
            volumes, gather_y, round_index, ny, iy, lambda at: (ix, at), gy_send_sem, gy_recv_sem
        )
        volumes = line_sum(
            volumes, gather_x, round_index, nx, ix, lambda at: (at, iy), gx_send_sem, gx_recv_sem
        )
        paired = volumes
        reach = 1
        while reach < band:
            other = jnp.where(
                (lane // reach) % 2 == 0,
                pltpu.roll(paired, size_z - reach, 1),
                pltpu.roll(paired, reach, 1),
            )
            paired = paired + other
            reach *= 2
        heavier = [paired[k : k + 1] > target for k in range(len(middles))]
        options = [(h, m) for h, m in zip(heavier, middles)]

        def descend(index, level, low, high):
            over, middle = options[index]
            if level == LEVELS - 1:
                return jnp.where(over, middle, low), jnp.where(over, high, middle)
            left = descend(2 * index + 1, level + 1, low, middle)
            right = descend(2 * index + 2, level + 1, middle, high)
            return jnp.where(over, right[0], left[0]), jnp.where(over, right[1], left[1])

        low_end, high_end = descend(0, 0, low_end, high_end)

    design_next[...] = candidate(jnp.sqrt(low_end * high_end))

    edge_finish(design_copies)
    edge_finish(scaled_copies)
    for (dx, dy), copy in zip(basis_steps, basis_copies):
        @pl.when(there(dx, dy))
        def _(copy=copy):
            copy.wait_send()
    for copy in pending:
        copy.wait_send()


def shards(nx, ny, design, passive, basis_pairs, supports, stiffness, mass_matrix, volume_fraction):
    size_x, size_y, size_z = design.shape
    pairs = basis_pairs.shape[0]
    regions = volume_fraction.shape[0]
    cells = size_x * size_y
    fields_n = 6 * pairs
    flat = (cells, size_z)
    vmem = pl.BlockSpec(memory_space=pltpu.VMEM)
    f32, bf16 = jnp.float32, jnp.bfloat16
    dma = pltpu.SemaphoreType.DMA
    outs = pl.pallas_call(
        functools.partial(kernel, nx, ny, size_x, size_y, size_z, pairs, regions),
        out_shape=(jax.ShapeDtypeStruct(flat, f32), jax.ShapeDtypeStruct(flat, f32)),
        in_specs=[vmem] * 7,
        out_specs=(vmem, vmem),
        scratch_shapes=[
            pltpu.VMEM((fields_n, (size_x + 1) * 2 * size_y, size_z), f32),
            pltpu.VMEM((fields_n, size_y, size_z), f32),
            pltpu.VMEM((fields_n, size_x, size_z), f32),
            pltpu.VMEM((fields_n, size_z), f32),
            pltpu.VMEM((fields_n, size_y, size_z), f32),
            pltpu.VMEM((fields_n, size_x, size_z), f32),
            pltpu.VMEM((fields_n, size_z), f32),
            pltpu.VMEM((2, 4, 2, size_x, size_z), f32),
            pltpu.VMEM((2, 8, 2, size_y, size_z), f32),
            pltpu.VMEM(((size_x + 4) * 3 * size_y, size_z), f32),
            pltpu.VMEM(flat, f32),
            pltpu.VMEM((48 * size_y, 24 * size_y), bf16),
            pltpu.VMEM((48 * size_y, 24 * size_y), bf16),
            pltpu.VMEM(flat, f32),
            pltpu.VMEM(flat, f32),
            pltpu.VMEM((2 * cells, size_z), f32),
            pltpu.VMEM((ROUNDS, ny, 8, size_z), f32),
            pltpu.VMEM((ROUNDS, nx, 8, size_z), f32),
            dma((3,)),
            dma((3,)),
            dma((2, 8)),
            dma((2, 8)),
            dma((ROUNDS, ny)),
            dma((ROUNDS, ny)),
            dma((ROUNDS, nx)),
            dma((ROUNDS, nx)),
        ],
        compiler_params=pltpu.CompilerParams(
            collective_id=0, has_side_effects=True, vmem_limit_bytes=48 * 1024 * 1024
        ),
        name="sensitivity_update",
    )(
        design.reshape(flat),
        passive.reshape(flat),
        basis_pairs.reshape(fields_n, cells, size_z),
        supports.reshape(flat),
        stiffness,
        mass_matrix,
        volume_fraction.reshape(1, regions),
    )
    return tuple(out.reshape(design.shape) for out in outs)


def solution(mesh):
    placed = (
        P("gx", "gy", None),
        P("gx", "gy", None),
        P(None, None, None, "gx", "gy", None),
        P("gx", "gy", None),
        P(),
        P(),
        P(),
    )
    return jax.shard_map(
        functools.partial(shards, mesh.shape["gx"], mesh.shape["gy"]),
        mesh=mesh,
        in_specs=placed,
        out_specs=(P("gx", "gy", None), P("gx", "gy", None)),
        check_vma=False,
    )
```

time: 356 us -> 40 us (0.11)
  blocking collectives: 241 us -> 0 us
  local copies, waits for them, and re-layouts: 50.1 us -> 6.7 us
  Pallas kernels: 0 us -> 32.2 us
  starting transfers between devices: 22.2 us -> 0 us
  waiting for transfers between devices: 17.8 us -> 0 us
  matrix products: 11.6 us -> 0 us
  other arithmetic: 8.48 us -> 0 us
    psum x6 -> x0, blocking collectives: 241 us -> none  [bisect_round(): volumes = lax.psum(partial_volumes, ('gx', 'gy'))]
    another operation x8 -> x0, local copies, waits for them, and re-layouts: 33.2 us -> none  [element_terms(): vectors.append(jnp.stack(row_list))]
    pallas_call x0 -> x1, Pallas kernels: none -> 32.2 us  [shards(): pl.pallas_call(functools.partial(kernel, nx, ny, size_x, size_y, size_z,...]
    ppermute x10 -> x0, starting transfers between devices: 22.2 us -> none  [the longest x4 14.4 us: with_halo(): lax.ppermute(tail, axis, [(i, (i + 1) % count) for i in range(ends)])]
    ppermute x10 -> x0, waiting for transfers between devices: 17.8 us -> none  [the longest x4 11.6 us: with_halo(): lax.ppermute(head, axis, [((i + 1) % count, i) for i in range(ends)])]
    dot_general x8 -> x0, matrix products: 11.6 us -> none  [the longest x4 7.01 us: element_terms(): jnp.dot(mass_matrix, adjoint_rows, precision=lax.Precision.HIGHEST)]
    slice x14 -> x0, local copies, waits for them, and re-layouts: 9.2 us -> none  [the longest x9 8.39 us: element_terms(): extended[pair_index, member, component, corner_x:corner_x + cells_x, corn...]
    unnamed x117 -> x16, local copies, waits for them, and re-layouts: 0.65 us -> 6.7 us
  transfers between devices with their start and end apart: 10 -> 0, of which waited for: 4 -> 0; matrix products, arithmetic and copies ran while one was open for 2% -> 0% of each run, Pallas kernels for 0% -> 0%
where the time goes in v1:
time: 40 us; the launch traced here: 39.6 us
  Pallas kernels  32.2 us (81%)
  local copies, waits for them, and re-layouts  6.7 us (17%)
  between operations  0.66 us (2%)
    pallas_call x1, Pallas kernels, shards(): pl.pallas_call(functools.partial(kernel, nx, ny, size_x, size_y, size_z,...  32.2 us
    unnamed x16, local copies, waits for them, and re-layouts  6.7 us

profile of v1, /device:TPU:0, one launch (start us, length us, event | category | flops | bytes accessed | tf_op | source)
XLA Modules:
  0.0 39.6 jit_solution(2314739770726597522)
XLA Ops:
  0.6 0.0 copy-start.6
  0.6 0.6 %copy-done.6 = f32[64]{0:T(128)S(1)} copy-done((f32[64]{0:T(128)S(1)}, f32[64]{0:T(128)}, u32[]{:S(2)}) %copy-start.6) | copy-done | bytes 280
  1.3 0.0 copy-start
  1.3 1.1 %copy-done = f32[4,2,3,8,8,128]{5,4,3,2,1,0:T(8,128)S(1)} copy-done((f32[4,2,3,8,8,128]{5,4,3,2,1,0:T(8,128)S(1)}, f32[4,2,3,8,8,128]{5,4,3,2,1,0:T(8,128)}, u32[]{:S(2)}) %copy-start) | copy-done | bytes 786456
  2.4 0.0 copy-start.1
  2.4 0.8 %copy-done.1 = f32[8,8,128]{2,1,0:T(8,128)S(1)} copy-done((f32[8,8,128]{2,1,0:T(8,128)S(1)}, f32[8,8,128]{2,1,0:T(8,128)}, u32[]{:S(2)}) %copy-start.1) | copy-done | bytes 32792
  3.2 0.0 copy-start.2
  3.2 0.8 %copy-done.2 = s32[8,8,128]{2,1,0:T(8,128)S(1)} copy-done((s32[8,8,128]{2,1,0:T(8,128)S(1)}, s32[8,8,128]{2,1,0:T(8,128)}, u32[]{:S(2)}) %copy-start.2) | copy-done | bytes 32792
  3.9 0.0 copy-start.3
  3.9 0.8 %copy-done.3 = s32[8,8,128]{2,1,0:T(8,128)S(1)} copy-done((s32[8,8,128]{2,1,0:T(8,128)S(1)}, s32[8,8,128]{2,1,0:T(8,128)}, u32[]{:S(2)}) %copy-start.3) | copy-done | bytes 32792
  4.7 0.0 copy-start.4
  4.7 0.7 %copy-done.4 = f32[24,24]{1,0:T(8,128)S(1)} copy-done((f32[24,24]{1,0:T(8,128)S(1)}, f32[24,24]{1,0:T(8,128)}, u32[]{:S(2)}) %copy-start.4) | copy-done | bytes 2328
  5.4 0.0 copy-start.5
  5.4 0.7 %copy-done.5 = f32[24,24]{1,0:T(8,128)S(1)} copy-done((f32[24,24]{1,0:T(8,128)S(1)}, f32[24,24]{1,0:T(8,128)}, u32[]{:S(2)}) %copy-start.5) | copy-done | bytes 2328
  6.1 32.2 %sensitivity_update.1 = (f32[64,128]{1,0:T(8,128)S(1)}, f32[64,128]{1,0:T(8,128)S(1)}) custom-call(f32[64,128]{1,0:T(8,128)S(1)} %bitcast.8, s32[64,128]{1,0:T(8,128)S(1)} %bitcast.9, f32[24,64,128]{2,1,0:T(8,128)S(1)} %bitcast.7, s32[64,128]{1,0:T(8,128)S(1)} %bitcast.10, f32[24,24]{1,0:T(8,128)S(1)} %copy-done.4, f32[24,24]{1,0:T(8,128)S(1)} %copy-done.5, ...), custom_call_target="tpu_custom_call" | custom-call | tf_op jit(solution)/shard_map/sensitivity_update/pallas_call | solution.py:422
  38.3 0.6 %copy.11 = f32[8,8,128]{2,1,0:T(8,128)} copy(f32[8,8,128]{2,1,0:T(8,128)S(1)} %bitcast.12) | data formatting | bytes 65536
  39.0 0.6 %copy.12 = f32[8,8,128]{2,1,0:T(8,128)} copy(f32[8,8,128]{2,1,0:T(8,128)S(1)} %bitcast.11) | data formatting | bytes 65536
Async XLA Ops:
  0.6 0.7 %copy-start.6 = (f32[64]{0:T(128)S(1)}, f32[64]{0:T(128)}, u32[]{:S(2)}) copy-start(f32[64]{0:T(128)} %param.13) | copy-start | bytes 772
  1.3 1.1 %copy-start = (f32[4,2,3,8,8,128]{5,4,3,2,1,0:T(8,128)S(1)}, f32[4,2,3,8,8,128]{5,4,3,2,1,0:T(8,128)}, u32[]{:S(2)}) copy-start(f32[4,2,3,8,8,128]{5,4,3,2,1,0:T(8,128)} %param.9) | copy-start | bytes 2359300
  2.4 0.8 %copy-start.1 = (f32[8,8,128]{2,1,0:T(8,128)S(1)}, f32[8,8,128]{2,1,0:T(8,128)}, u32[]{:S(2)}) copy-start(f32[8,8,128]{2,1,0:T(8,128)} %param.7) | copy-start | bytes 98308
  3.2 0.8 %copy-start.2 = (s32[8,8,128]{2,1,0:T(8,128)S(1)}, s32[8,8,128]{2,1,0:T(8,128)}, u32[]{:S(2)}) copy-start(s32[8,8,128]{2,1,0:T(8,128)} %param.8) | copy-start | bytes 98308
  3.9 0.8 %copy-start.3 = (s32[8,8,128]{2,1,0:T(8,128)S(1)}, s32[8,8,128]{2,1,0:T(8,128)}, u32[]{:S(2)}) copy-start(s32[8,8,128]{2,1,0:T(8,128)} %param.10) | copy-start | bytes 98308
  4.7 0.7 %copy-start.4 = (f32[24,24]{1,0:T(8,128)S(1)}, f32[24,24]{1,0:T(8,128)}, u32[]{:S(2)}) copy-start(f32[24,24]{1,0:T(8,128)} %stiffness.1) | copy-start | bytes 6916
  5.4 0.7 %copy-start.5 = (f32[24,24]{1,0:T(8,128)S(1)}, f32[24,24]{1,0:T(8,128)}, u32[]{:S(2)}) copy-start(f32[24,24]{1,0:T(8,128)} %mass_matrix.1) | copy-start | bytes 6916

commit v2 on v1

--- a/solution.py
+++ b/solution.py
@@ -3,6 +3,7 @@
 
 import jax
 import jax.numpy as jnp
+import numpy as np
 from jax import lax
 from jax.experimental import pallas as pl
 from jax.experimental.pallas import tpu as pltpu
@@ -11,10 +12,25 @@
 PENALTY_SCALE = 3.0 * (1.0 - 0.001)
 OMEGA_SQUARED = 0.5
 MOVE_LIMIT = 0.2
-LEVELS = 3
-ROUNDS = 2
+BISECT = 6
+TRIALS = 2**BISECT
 MESH = pl.DeviceIdType.MESH
 AROUND = ((-1, 0), (1, 0), (0, -1), (0, 1), (-1, -1), (-1, 1), (1, -1), (1, 1))
+
+
+def tree_ends():
+    ends = [np.float32(1e-4), np.float32(1e4)]
+    for _ in range(BISECT):
+        inner = [np.sqrt(p * q) for p, q in zip(ends, ends[1:])]
+        ends = [ends[0]] + [e for pair in zip(inner, ends[1:]) for e in pair]
+    return ends
+
+
+ENDS = tree_ends()
+INVERSE_MIDDLES = [float(np.float32(1.0) / np.sqrt(e)) for e in ENDS[1:-1]]
+INVERSE_LEAVES = [
+    float(np.float32(1.0) / np.sqrt(np.sqrt(p * q))) for p, q in zip(ENDS, ENDS[1:])
+]
 
 
 def opposite(slot):
@@ -60,13 +76,15 @@
 
 def kernel(
     nx, ny, size_x, size_y, size_z, pairs, regions,
+    design_hbm, passive_hbm, basis_hbm, supports_hbm, stiffness_hbm, mass_hbm, fraction_hbm,
+    sensitivity, design_next,
     design, passive, basis, supports, stiffness, mass_matrix, fraction,
-    sensitivity, design_next,
     fields, send_x, send_y, send_c, recv_x, recv_y, recv_c,
     edge_send, edge_recv, wide, scaled, weights_hi, weights_lo, weight_sum, physical, energy,
-    gather_y, gather_x,
+    share_send, share_recv, gather_x, gather_y, leaf_table,
+    load_sem,
     basis_send_sem, basis_recv_sem, halo_send_sem, halo_recv_sem,
-    gy_send_sem, gy_recv_sem, gx_send_sem, gx_recv_sem,
+    share_send_sem, share_recv_sem, gx_send_sem, gx_recv_sem, gy_send_sem, gy_recv_sem,
 ):
     ix, iy = lax.axis_index("gx"), lax.axis_index("gy")
     pitch = 2 * size_y
@@ -87,6 +105,18 @@
         def _(dx=dx, dy=dy):
             pl.semaphore_signal(barrier, inc=1, device_id=(ix + dx, iy + dy), device_id_type=MESH)
     corners = sum(there(dx, dy).astype(jnp.int32) for dx, dy in AROUND[4:])
+
+    loads = [
+        pltpu.make_async_copy(src, dst, load_sem.at[k])
+        for k, (src, dst) in enumerate((
+            (supports_hbm, supports), (basis_hbm, basis), (design_hbm, design), (passive_hbm, passive),
+            (stiffness_hbm, stiffness), (mass_hbm, mass_matrix), (fraction_hbm, fraction),
+        ))
+    ]
+    for load in loads:
+        load.start()
+    for load in loads:
+        load.wait()
 
     free = 1.0 - supports[...].astype(jnp.float32)
     send_x[...] = basis[:, 0:size_y, :] * free[0:size_y][None]
@@ -228,6 +258,35 @@
     for x, tile in enumerate(stencil(inside, size_x)):
         weight_sum[pl.ds(x * size_y, size_y), :] = tile
 
+    band = size_z // regions
+    width, group_rows = size_z // ny, TRIALS // ny
+    lane = lax.broadcasted_iota(jnp.int32, (group_rows, size_z), 1)
+    lane8 = lax.broadcasted_iota(jnp.int32, (8, size_z), 1)
+    slot_row = lax.broadcasted_iota(jnp.int32, (8, size_z), 0)
+    group = lane // width
+    pick = (
+        lax.broadcasted_iota(jnp.int32, (regions, size_z), 1) // band
+        == lax.broadcasted_iota(jnp.int32, (regions, size_z), 0)
+    ).astype(jnp.float32).astype(jnp.bfloat16)
+    rest = jnp.broadcast_to(fraction[...], (8, regions))
+    target = jnp.zeros((8, size_z), jnp.float32)
+    for _ in range(3):
+        piece = rest.astype(jnp.bfloat16)
+        target = target + jnp.dot(piece, pick, preferred_element_type=jnp.float32)
+        rest = rest - piece.astype(jnp.float32)
+    target = target * float(grid_x * grid_y * band)
+    own_target = jnp.where(lane8 // width == iy, target, 0.0)
+    reach = width
+    while reach < size_z:
+        own_target = own_target + pltpu.roll(own_target, reach, 1)
+        reach *= 2
+    for r in range(group_rows):
+        line = jnp.full((1, size_z), INVERSE_LEAVES[0], jnp.float32)
+        for g in range(ny):
+            j = min(g * group_rows + r + 1, TRIALS - 1)
+            line = jnp.where(lane8[0:1] // width == g, INVERSE_LEAVES[j], line)
+        leaf_table[pl.ds(r, 1), :] = line
+
     edge_receive(design_copies, 0)
     assemble(design, 0)
     for x, tile in enumerate(stencil(wide_rows, size_x)):
@@ -308,42 +367,58 @@
 
     value = design[...]
     gain = value * jnp.sqrt(jnp.maximum(-sensitivity[...], 0.0))
-    floor_value = jnp.maximum(value - MOVE_LIMIT, 0.0)
-    ceiling = jnp.minimum(value + MOVE_LIMIT, 1.0)
-
-    def candidate(multiplier):
-        trial = gain * (1.0 / jnp.sqrt(multiplier))
-        return jnp.where(solid, 1.0, jnp.minimum(ceiling, jnp.maximum(floor_value, trial)))
-
-    band = size_z // regions
-    pick = (
-        lax.broadcasted_iota(jnp.int32, (regions, size_z), 1) // band
-        == lax.broadcasted_iota(jnp.int32, (regions, size_z), 0)
-    ).astype(jnp.float32).astype(jnp.bfloat16)
-    rest = jnp.broadcast_to(fraction[...], (8, regions))
-    target = jnp.zeros((8, size_z), jnp.float32)
-    for _ in range(3):
-        piece = rest.astype(jnp.bfloat16)
-        target = target + jnp.dot(piece, pick, preferred_element_type=jnp.float32)
-        rest = rest - piece.astype(jnp.float32)
-    target = target[0:1] * float(grid_x * grid_y * band)
-
-    lane = lax.broadcasted_iota(jnp.int32, (8, size_z), 1)
-    slot_row = lax.broadcasted_iota(jnp.int32, (8, size_z), 0)
-    low_end = jnp.full((1, size_z), 1e-4, jnp.float32)
-    high_end = jnp.full((1, size_z), 1e4, jnp.float32)
+    floor_value = jnp.where(solid, 1.0, jnp.maximum(value - MOVE_LIMIT, 0.0))
+    ceiling = jnp.where(solid, 1.0, jnp.minimum(value + MOVE_LIMIT, 1.0))
+
+    def candidate(inverse_root):
+        return jnp.minimum(ceiling, jnp.maximum(floor_value, gain * inverse_root))
+
+    def total_over_x(j):
+        trial = candidate(INVERSE_MIDDLES[j])
+        return functools.reduce(
+            lambda p, q: p + q, [trial[x * size_y : (x + 1) * size_y] for x in range(size_x)]
+        )
+
+    volumes = []
+    for first in range(0, TRIALS, 8):
+        tiles = [
+            total_over_x(j) if j < TRIALS - 1 else jnp.zeros((8, size_z), jnp.float32)
+            for j in range(first, first + 8)
+        ]
+        reach = 4
+        while reach:
+            lower = (slot_row & reach) == 0
+            tiles = [
+                jnp.where(lower, p, q)
+                + jnp.where(lower, pltpu.roll(p, 8 - reach, 0), pltpu.roll(q, reach, 0))
+                for p, q in zip(tiles[:reach], tiles[reach:])
+            ]
+            reach //= 2
+        volumes.append(tiles[0])
+    volumes = jnp.concatenate(volumes, axis=0)
+
+    for q in range(ny):
+        packed = jnp.zeros((group_rows, size_z), jnp.float32)
+        for g in range(ny):
+            part = volumes[g * group_rows : (g + 1) * group_rows]
+            turn = (width * (g - q)) % size_z
+            if turn:
+                part = pltpu.roll(part, turn, 1)
+            packed = jnp.where(group == g, part, packed)
+        share_send[q] = packed
+    share_recv[pl.ds(iy, 1)] = share_send[pl.ds(iy, 1)]
     pending = []
 
-    def line_sum(part, buffer, round_index, count, me, target_of, send_sem, recv_sem):
-        buffer[round_index, pl.ds(me, 1)] = part[None]
+    def along(count, me, place, source, buffer, send_sem, recv_sem):
         copies = []
         for step in range(1, count):
+            peer = lax.rem(me + step, count)
             copy = pltpu.make_async_remote_copy(
-                src_ref=buffer.at[round_index, me],
-                dst_ref=buffer.at[round_index, me],
-                send_sem=send_sem.at[round_index, step],
-                recv_sem=recv_sem.at[round_index, step],
-                device_id=target_of(lax.rem(me + step, count)),
+                src_ref=source(peer),
+                dst_ref=buffer.at[me],
+                send_sem=send_sem.at[step],
+                recv_sem=recv_sem.at[step],
+                device_id=place(peer),
                 device_id_type=MESH,
             )
             copy.start()
@@ -351,53 +426,33 @@
         for copy in copies:
             copy.wait_recv()
         pending.extend(copies)
-        return functools.reduce(lambda a, b: a + b, [buffer[round_index, k] for k in range(count)])
-
-    for round_index in range(ROUNDS):
-        nodes = [(low_end, high_end)]
-        middles = []
-        for level in range(LEVELS):
-            following = []
-            for node_low, node_high in nodes:
-                middle = jnp.sqrt(node_low * node_high)
-                middles.append(middle)
-                following += [(node_low, middle), (middle, node_high)]
-            nodes = following
-        volumes = jnp.zeros((8, size_z), jnp.float32)
-        for k, middle in enumerate(middles):
-            trial = candidate(middle).reshape(size_x, size_y, size_z)
-            column = jnp.sum(jnp.sum(trial, axis=0), axis=0, keepdims=True)
-            volumes = jnp.where(slot_row == k, column, volumes)
-        volumes = line_sum(
-            volumes, gather_y, round_index, ny, iy, lambda at: (ix, at), gy_send_sem, gy_recv_sem
-        )
-        volumes = line_sum(
-            volumes, gather_x, round_index, nx, ix, lambda at: (at, iy), gx_send_sem, gx_recv_sem
-        )
-        paired = volumes
-        reach = 1
-        while reach < band:
-            other = jnp.where(
-                (lane // reach) % 2 == 0,
-                pltpu.roll(paired, size_z - reach, 1),
-                pltpu.roll(paired, reach, 1),
-            )
-            paired = paired + other
-            reach *= 2
-        heavier = [paired[k : k + 1] > target for k in range(len(middles))]
-        options = [(h, m) for h, m in zip(heavier, middles)]
-
-        def descend(index, level, low, high):
-            over, middle = options[index]
-            if level == LEVELS - 1:
-                return jnp.where(over, middle, low), jnp.where(over, high, middle)
-            left = descend(2 * index + 1, level + 1, low, middle)
-            right = descend(2 * index + 2, level + 1, middle, high)
-            return jnp.where(over, right[0], left[0]), jnp.where(over, right[1], left[1])
-
-        low_end, high_end = descend(0, 0, low_end, high_end)
-
-    design_next[...] = candidate(jnp.sqrt(low_end * high_end))
+
+    along(ny, iy, lambda at: (ix, at), lambda at: share_send.at[at], share_recv, share_send_sem, share_recv_sem)
+    share = functools.reduce(lambda p, q: p + q, [share_recv[k] for k in range(ny)])
+    gather_x[pl.ds(ix, 1)] = share[None]
+    along(nx, ix, lambda at: (at, iy), lambda at: gather_x.at[ix], gather_x, gx_send_sem, gx_recv_sem)
+    share = functools.reduce(lambda p, q: p + q, [gather_x[k] for k in range(nx)])
+
+    reach = 1
+    while reach < band:
+        share = share + jnp.where(
+            (lane // reach) % 2 == 0,
+            pltpu.roll(share, size_z - reach, 1),
+            pltpu.roll(share, reach, 1),
+        )
+        reach *= 2
+    chosen = jnp.where(share > own_target[0:1], leaf_table[...], INVERSE_LEAVES[0])
+    chosen = jnp.min(chosen, axis=0, keepdims=True)
+    reach = width
+    while reach < size_z:
+        chosen = jnp.minimum(chosen, pltpu.roll(chosen, reach, 1))
+        reach *= 2
+    gather_y[pl.ds(iy, 1)] = jnp.broadcast_to(chosen, (8, size_z))[None]
+    along(ny, iy, lambda at: (ix, at), lambda at: gather_y.at[iy], gather_y, gy_send_sem, gy_recv_sem)
+    multiplier = gather_y[0]
+    for q in range(1, ny):
+        multiplier = jnp.where(lane8 // width == q, gather_y[q], multiplier)
+    design_next[...] = candidate(multiplier[0:1])
 
     edge_finish(design_copies)
     edge_finish(scaled_copies)
@@ -422,9 +477,16 @@
     outs = pl.pallas_call(
         functools.partial(kernel, nx, ny, size_x, size_y, size_z, pairs, regions),
         out_shape=(jax.ShapeDtypeStruct(flat, f32), jax.ShapeDtypeStruct(flat, f32)),
-        in_specs=[vmem] * 7,
+        in_specs=[pl.BlockSpec(memory_space=pltpu.HBM)] * 7,
         out_specs=(vmem, vmem),
         scratch_shapes=[
+            pltpu.VMEM(flat, f32),
+            pltpu.VMEM(flat, jnp.int32),
+            pltpu.VMEM((fields_n, cells, size_z), f32),
+            pltpu.VMEM(flat, jnp.int32),
+            pltpu.VMEM(stiffness.shape, f32),
+            pltpu.VMEM(mass_matrix.shape, f32),
+            pltpu.VMEM((1, regions), f32),
             pltpu.VMEM((fields_n, (size_x + 1) * 2 * size_y, size_z), f32),
             pltpu.VMEM((fields_n, size_y, size_z), f32),
             pltpu.VMEM((fields_n, size_x, size_z), f32),
@@ -441,16 +503,22 @@
             pltpu.VMEM(flat, f32),
             pltpu.VMEM(flat, f32),
             pltpu.VMEM((2 * cells, size_z), f32),
-            pltpu.VMEM((ROUNDS, ny, 8, size_z), f32),
-            pltpu.VMEM((ROUNDS, nx, 8, size_z), f32),
+            pltpu.VMEM((ny, TRIALS // ny, size_z), f32),
+            pltpu.VMEM((ny, TRIALS // ny, size_z), f32),
+            pltpu.VMEM((nx, TRIALS // ny, size_z), f32),
+            pltpu.VMEM((ny, 8, size_z), f32),
+            pltpu.VMEM((TRIALS // ny, size_z), f32),
+            dma((7,)),
             dma((3,)),
             dma((3,)),
             dma((2, 8)),
             dma((2, 8)),
-            dma((ROUNDS, ny)),
-            dma((ROUNDS, ny)),
-            dma((ROUNDS, nx)),
-            dma((ROUNDS, nx)),
+            dma((ny,)),
+            dma((ny,)),
+            dma((nx,)),
+            dma((nx,)),
+            dma((ny,)),
+            dma((ny,)),
         ],
         compiler_params=pltpu.CompilerParams(
             collective_id=0, has_side_effects=True, vmem_limit_bytes=48 * 1024 * 1024

time: 40 us -> 36.4 us (0.910)
  Pallas kernels: 32.2 us -> 28.6 us
    pallas_call x1, Pallas kernels: 32.2 us -> 28.6 us  [shards(): pl.pallas_call(functools.partial(kernel, nx, ny, size_x, size_y, size_z,...]
where the time goes in v2:
time: 36.4 us; the launch traced here: 35.9 us
  Pallas kernels  28.6 us (79%)
  local copies, waits for them, and re-layouts  6.7 us (18%)
  between operations  0.66 us (2%)
    pallas_call x1, Pallas kernels, shards(): pl.pallas_call(functools.partial(kernel, nx, ny, size_x, size_y, size_z,...  28.6 us
    unnamed x16, local copies, waits for them, and re-layouts  6.7 us

profile of v2, /device:TPU:0, one launch (start us, length us, event | category | flops | bytes accessed | tf_op | source)
XLA Modules:
  0.0 35.9 jit_solution(15008968216897548013)
XLA Ops:
  0.6 0.0 copy-start.6
  0.6 0.6 %copy-done.6 = f32[64]{0:T(128)S(1)} copy-done((f32[64]{0:T(128)S(1)}, f32[64]{0:T(128)}, u32[]{:S(2)}) %copy-start.6) | copy-done | bytes 280
  1.3 0.0 copy-start
  1.3 1.1 %copy-done = f32[4,2,3,8,8,128]{5,4,3,2,1,0:T(8,128)S(1)} copy-done((f32[4,2,3,8,8,128]{5,4,3,2,1,0:T(8,128)S(1)}, f32[4,2,3,8,8,128]{5,4,3,2,1,0:T(8,128)}, u32[]{:S(2)}) %copy-start) | copy-done | bytes 786456
  2.4 0.0 copy-start.1
  2.4 0.8 %copy-done.1 = f32[8,8,128]{2,1,0:T(8,128)S(1)} copy-done((f32[8,8,128]{2,1,0:T(8,128)S(1)}, f32[8,8,128]{2,1,0:T(8,128)}, u32[]{:S(2)}) %copy-start.1) | copy-done | bytes 32792
  3.2 0.0 copy-start.2
  3.2 0.8 %copy-done.2 = s32[8,8,128]{2,1,0:T(8,128)S(1)} copy-done((s32[8,8,128]{2,1,0:T(8,128)S(1)}, s32[8,8,128]{2,1,0:T(8,128)}, u32[]{:S(2)}) %copy-start.2) | copy-done | bytes 32792
  3.9 0.0 copy-start.3
  3.9 0.8 %copy-done.3 = s32[8,8,128]{2,1,0:T(8,128)S(1)} copy-done((s32[8,8,128]{2,1,0:T(8,128)S(1)}, s32[8,8,128]{2,1,0:T(8,128)}, u32[]{:S(2)}) %copy-start.3) | copy-done | bytes 32792
  4.7 0.0 copy-start.4
  4.7 0.7 %copy-done.4 = f32[24,24]{1,0:T(8,128)S(1)} copy-done((f32[24,24]{1,0:T(8,128)S(1)}, f32[24,24]{1,0:T(8,128)}, u32[]{:S(2)}) %copy-start.4) | copy-done | bytes 2328
  5.4 0.0 copy-start.5
  5.4 0.7 %copy-done.5 = f32[24,24]{1,0:T(8,128)S(1)} copy-done((f32[24,24]{1,0:T(8,128)S(1)}, f32[24,24]{1,0:T(8,128)}, u32[]{:S(2)}) %copy-start.5) | copy-done | bytes 2328
  6.1 28.6 %sensitivity_update.1 = (f32[64,128]{1,0:T(8,128)S(1)}, f32[64,128]{1,0:T(8,128)S(1)}) custom-call(f32[64,128]{1,0:T(8,128)S(1)} %bitcast.8, s32[64,128]{1,0:T(8,128)S(1)} %bitcast.9, f32[24,64,128]{2,1,0:T(8,128)S(1)} %bitcast.7, s32[64,128]{1,0:T(8,128)S(1)} %bitcast.10, f32[24,24]{1,0:T(8,128)S(1)} %copy-done.4, f32[24,24]{1,0:T(8,128)S(1)} %copy-done.5, ...), custom_call_target="tpu_custom_call" | custom-call | tf_op jit(solution)/shard_map/sensitivity_update/pallas_call | solution.py:477
  34.7 0.6 %copy.11 = f32[8,8,128]{2,1,0:T(8,128)} copy(f32[8,8,128]{2,1,0:T(8,128)S(1)} %bitcast.12) | data formatting | bytes 65536
  35.3 0.6 %copy.12 = f32[8,8,128]{2,1,0:T(8,128)} copy(f32[8,8,128]{2,1,0:T(8,128)S(1)} %bitcast.11) | data formatting | bytes 65536
Async XLA Ops:
  0.6 0.7 %copy-start.6 = (f32[64]{0:T(128)S(1)}, f32[64]{0:T(128)}, u32[]{:S(2)}) copy-start(f32[64]{0:T(128)} %param.13) | copy-start | bytes 772
  1.3 1.1 %copy-start = (f32[4,2,3,8,8,128]{5,4,3,2,1,0:T(8,128)S(1)}, f32[4,2,3,8,8,128]{5,4,3,2,1,0:T(8,128)}, u32[]{:S(2)}) copy-start(f32[4,2,3,8,8,128]{5,4,3,2,1,0:T(8,128)} %param.9) | copy-start | bytes 2359300
  2.4 0.8 %copy-start.1 = (f32[8,8,128]{2,1,0:T(8,128)S(1)}, f32[8,8,128]{2,1,0:T(8,128)}, u32[]{:S(2)}) copy-start(f32[8,8,128]{2,1,0:T(8,128)} %param.7) | copy-start | bytes 98308
  3.2 0.8 %copy-start.2 = (s32[8,8,128]{2,1,0:T(8,128)S(1)}, s32[8,8,128]{2,1,0:T(8,128)}, u32[]{:S(2)}) copy-start(s32[8,8,128]{2,1,0:T(8,128)} %param.8) | copy-start | bytes 98308
  3.9 0.8 %copy-start.3 = (s32[8,8,128]{2,1,0:T(8,128)S(1)}, s32[8,8,128]{2,1,0:T(8,128)}, u32[]{:S(2)}) copy-start(s32[8,8,128]{2,1,0:T(8,128)} %param.10) | copy-start | bytes 98308
  4.7 0.7 %copy-start.4 = (f32[24,24]{1,0:T(8,128)S(1)}, f32[24,24]{1,0:T(8,128)}, u32[]{:S(2)}) copy-start(f32[24,24]{1,0:T(8,128)} %stiffness_hbm.1) | copy-start | bytes 6916
  5.4 0.7 %copy-start.5 = (f32[24,24]{1,0:T(8,128)S(1)}, f32[24,24]{1,0:T(8,128)}, u32[]{:S(2)}) copy-start(f32[24,24]{1,0:T(8,128)} %mass_hbm.1) | copy-start | bytes 6916

commit v3 on v2

--- a/solution.py
+++ b/solution.py
@@ -77,12 +77,12 @@
 def kernel(
     nx, ny, size_x, size_y, size_z, pairs, regions,
     design_hbm, passive_hbm, basis_hbm, supports_hbm, stiffness_hbm, mass_hbm, fraction_hbm,
-    sensitivity, design_next,
-    design, passive, basis, supports, stiffness, mass_matrix, fraction,
+    benefit_hbm, chosen_out,
+    benefit, design, passive, basis, supports, stiffness, mass_matrix, fraction,
     fields, send_x, send_y, send_c, recv_x, recv_y, recv_c,
     edge_send, edge_recv, wide, scaled, weights_hi, weights_lo, weight_sum, physical, energy,
     share_send, share_recv, gather_x, gather_y, leaf_table,
-    load_sem,
+    load_sem, out_sem,
     basis_send_sem, basis_recv_sem, halo_send_sem, halo_recv_sem,
     share_send_sem, share_recv_sem, gx_send_sem, gx_recv_sem, gy_send_sem, gy_recv_sem,
 ):
@@ -124,7 +124,7 @@
     for f in range(6 * pairs):
         rows = basis[f, pl.ds(0, size_x, stride=size_y), :] * free_y
         send_y[f] = rows
-        send_c[pl.ds(f, 1), :] = rows[0:1]
+        send_c[f // 6, pl.ds(f % 6, 1), :] = rows[0:1]
 
     def pack_edges(source, which):
         for x in range(2):
@@ -198,40 +198,18 @@
 
     pack_edges(design, 0)
 
-    pl.semaphore_wait(barrier, (nx - 1) + (ny - 1) + corners)
-
-    design_copies = edge_copies(0)
-    edge_start(design_copies)
-    basis_steps = ((-1, 0), (0, -1), (-1, -1))
-    basis_copies = [
-        pltpu.make_async_remote_copy(
-            src_ref=src, dst_ref=dst, send_sem=basis_send_sem.at[k], recv_sem=basis_recv_sem.at[k],
-            device_id=(ix + dx, iy + dy), device_id_type=MESH,
-        )
-        for k, ((dx, dy), src, dst) in enumerate(
-            zip(basis_steps, (send_x, send_y, send_c), (recv_x, recv_y, recv_c))
-        )
-    ]
-    for (dx, dy), copy in zip(basis_steps, basis_copies):
-        @pl.when(there(dx, dy))
-        def _(copy=copy):
-            copy.start()
-
-    for x in range(size_x):
-        fields[:, x * pitch : x * pitch + size_y, :] = (
-            basis[:, x * size_y : (x + 1) * size_y, :] * free[x * size_y : (x + 1) * size_y][None]
-        )
-
+    grid_x, grid_y = nx * size_x, ny * size_y
     wide_n, narrow_n = 24 * size_y, 24
+    bits_y = size_y.bit_length() - 1
     row = lax.broadcasted_iota(jnp.int32, (wide_n, narrow_n), 0)
     col = lax.broadcasted_iota(jnp.int32, (wide_n, narrow_n), 1)
-    expand = (row // size_y == col).astype(jnp.float32).astype(jnp.bfloat16)
+    expand = (lax.shift_right_logical(row, bits_y) == col).astype(jnp.float32).astype(jnp.bfloat16)
     row_t = lax.broadcasted_iota(jnp.int32, (narrow_n, wide_n), 0)
     col_t = lax.broadcasted_iota(jnp.int32, (narrow_n, wide_n), 1)
-    expand_t = (col_t // size_y == row_t).astype(jnp.float32).astype(jnp.bfloat16)
+    expand_t = (lax.shift_right_logical(col_t, bits_y) == row_t).astype(jnp.float32).astype(jnp.bfloat16)
     same = (
-        lax.broadcasted_iota(jnp.int32, (wide_n, wide_n), 0) % size_y
-        == lax.broadcasted_iota(jnp.int32, (wide_n, wide_n), 1) % size_y
+        lax.broadcasted_iota(jnp.int32, (wide_n, wide_n), 0) & (size_y - 1)
+        == lax.broadcasted_iota(jnp.int32, (wide_n, wide_n), 1) & (size_y - 1)
     )
 
     def spread_matrix(piece):
@@ -245,18 +223,6 @@
         low = (value - high.astype(jnp.float32)).astype(jnp.bfloat16)
         weights_hi[pl.ds(k * wide_n, wide_n), :] = spread_matrix(high)
         weights_lo[pl.ds(k * wide_n, wide_n), :] = spread_matrix(low)
-
-    row_y = lax.broadcasted_iota(jnp.int32, (size_y, size_z), 0)
-    grid_x, grid_y = nx * size_x, ny * size_y
-
-    def inside(plane, oy):
-        at_x = ix * size_x + plane - 2
-        at_y = row_y + (iy * size_y + oy)
-        ok = (at_y >= 0) & (at_y < grid_y) & (at_x >= 0) & (at_x < grid_x)
-        return jnp.where(ok, 1.0, 0.0)
-
-    for x, tile in enumerate(stencil(inside, size_x)):
-        weight_sum[pl.ds(x * size_y, size_y), :] = tile
 
     band = size_z // regions
     width, group_rows = size_z // ny, TRIALS // ny
@@ -268,7 +234,7 @@
         lax.broadcasted_iota(jnp.int32, (regions, size_z), 1) // band
         == lax.broadcasted_iota(jnp.int32, (regions, size_z), 0)
     ).astype(jnp.float32).astype(jnp.bfloat16)
-    rest = jnp.broadcast_to(fraction[...], (8, regions))
+    rest = jnp.broadcast_to(fraction[...].reshape(1, regions), (8, regions))
     target = jnp.zeros((8, size_z), jnp.float32)
     for _ in range(3):
         piece = rest.astype(jnp.bfloat16)
@@ -287,29 +253,75 @@
             line = jnp.where(lane8[0:1] // width == g, INVERSE_LEAVES[j], line)
         leaf_table[pl.ds(r, 1), :] = line
 
+    pl.semaphore_wait(barrier, (nx - 1) + (ny - 1) + corners)
+
+    design_copies = edge_copies(0)
+    edge_start(design_copies)
+    basis_steps = ((-1, 0), (0, -1), (-1, -1))
+    def basis_copies(pair):
+        rows = pl.ds(pair * 6, 6)
+        return [
+            pltpu.make_async_remote_copy(
+                src_ref=src.at[rows] if k < 2 else src.at[pair],
+                dst_ref=dst.at[rows] if k < 2 else dst.at[pair],
+                send_sem=basis_send_sem.at[pair, k],
+                recv_sem=basis_recv_sem.at[pair, k],
+                device_id=(ix + dx, iy + dy),
+                device_id_type=MESH,
+            )
+            for k, ((dx, dy), src, dst) in enumerate(
+                zip(basis_steps, (send_x, send_y, send_c), (recv_x, recv_y, recv_c))
+            )
+        ]
+
+    for pair in range(pairs):
+        for (dx, dy), copy in zip(basis_steps, basis_copies(pair)):
+            @pl.when(there(dx, dy))
+            def _(copy=copy):
+                copy.start()
+
+    for x in range(size_x):
+        fields[:, x * pitch : x * pitch + size_y, :] = (
+            basis[:, x * size_y : (x + 1) * size_y, :] * free[x * size_y : (x + 1) * size_y][None]
+        )
+
+    row_y = lax.broadcasted_iota(jnp.int32, (size_y, size_z), 0)
+
+    def inside(plane, oy):
+        at_x = ix * size_x + plane - 2
+        at_y = row_y + (iy * size_y + oy)
+        ok = (at_y >= 0) & (at_y < grid_y) & (at_x >= 0) & (at_x < grid_x)
+        return jnp.where(ok, 1.0, 0.0)
+
+    for x, tile in enumerate(stencil(inside, size_x)):
+        weight_sum[pl.ds(x * size_y, size_y), :] = tile
+
     edge_receive(design_copies, 0)
     assemble(design, 0)
     for x, tile in enumerate(stencil(wide_rows, size_x)):
         at = pl.ds(x * size_y, size_y)
         physical[at, :] = jnp.where(passive[at, :] == 1, 1.0, tile / weight_sum[at, :])
 
-    for (dx, dy), copy, buffer in zip(basis_steps, basis_copies, (recv_x, recv_y, recv_c)):
-        @pl.when(there(-dx, -dy))
-        def _(copy=copy):
-            copy.wait_recv()
-
-        @pl.when(jnp.logical_not(there(-dx, -dy)))
-        def _(buffer=buffer):
-            buffer[...] = jnp.zeros(buffer.shape, jnp.float32)
-
-    fields[:, size_x * pitch : size_x * pitch + size_y, :] = recv_x[...]
-    for f in range(6 * pairs):
-        fields[f, pl.ds(size_y, size_x, stride=pitch), :] = recv_y[f]
-        fields[f, pl.ds(size_x * pitch + size_y, 1), :] = recv_c[pl.ds(f, 1), :]
-
     energy[...] = jnp.zeros((2 * cells, size_z), jnp.float32)
 
     def pair_step(pair, carry):
+        rows = pl.ds(pair * 6, 6)
+        buffers = (recv_x.at[rows], recv_y.at[rows], recv_c.at[pair])
+        for (dx, dy), copy, buffer in zip(basis_steps, basis_copies(pair), buffers):
+            @pl.when(there(-dx, -dy))
+            def _(copy=copy):
+                copy.wait_recv()
+
+            @pl.when(jnp.logical_not(there(-dx, -dy)))
+            def _(buffer=buffer):
+                buffer[...] = jnp.zeros(buffer.shape, jnp.float32)
+
+        fields[rows, size_x * pitch : size_x * pitch + size_y, :] = recv_x[rows]
+        for k in range(6):
+            f = pair * 6 + k
+            fields[f, pl.ds(size_y, size_x, stride=pitch), :] = recv_y[f]
+            fields[f, pl.ds(size_x * pitch + size_y, 1), :] = recv_c[pair, pl.ds(k, 1), :]
+
         def corner_tiles(member):
             tiles = {}
             for c in range(3):
@@ -363,10 +375,12 @@
     edge_receive(scaled_copies, 1)
     assemble(scaled, 1)
     for x, tile in enumerate(stencil(wide_rows, size_x)):
-        sensitivity[pl.ds(x * size_y, size_y), :] = tile
+        benefit[pl.ds(x * size_y, size_y), :] = -tile
+    benefit_out = pltpu.make_async_copy(benefit, benefit_hbm, out_sem)
+    benefit_out.start()
 
     value = design[...]
-    gain = value * jnp.sqrt(jnp.maximum(-sensitivity[...], 0.0))
+    gain = value * jnp.sqrt(jnp.maximum(benefit[...], 0.0))
     floor_value = jnp.where(solid, 1.0, jnp.maximum(value - MOVE_LIMIT, 0.0))
     ceiling = jnp.where(solid, 1.0, jnp.minimum(value + MOVE_LIMIT, 1.0))
 
@@ -452,14 +466,16 @@
     multiplier = gather_y[0]
     for q in range(1, ny):
         multiplier = jnp.where(lane8 // width == q, gather_y[q], multiplier)
-    design_next[...] = candidate(multiplier[0:1])
+    chosen_out[...] = multiplier
+    benefit_out.wait()
 
     edge_finish(design_copies)
     edge_finish(scaled_copies)
-    for (dx, dy), copy in zip(basis_steps, basis_copies):
-        @pl.when(there(dx, dy))
-        def _(copy=copy):
-            copy.wait_send()
+    for pair in range(pairs):
+        for (dx, dy), copy in zip(basis_steps, basis_copies(pair)):
+            @pl.when(there(dx, dy))
+            def _(copy=copy):
+                copy.wait_send()
     for copy in pending:
         copy.wait_send()
 
@@ -474,26 +490,27 @@
     vmem = pl.BlockSpec(memory_space=pltpu.VMEM)
     f32, bf16 = jnp.float32, jnp.bfloat16
     dma = pltpu.SemaphoreType.DMA
-    outs = pl.pallas_call(
+    negated, inverse_root = pl.pallas_call(
         functools.partial(kernel, nx, ny, size_x, size_y, size_z, pairs, regions),
-        out_shape=(jax.ShapeDtypeStruct(flat, f32), jax.ShapeDtypeStruct(flat, f32)),
+        out_shape=(jax.ShapeDtypeStruct(flat, f32), jax.ShapeDtypeStruct((size_y, size_z), f32)),
         in_specs=[pl.BlockSpec(memory_space=pltpu.HBM)] * 7,
-        out_specs=(vmem, vmem),
+        out_specs=(pl.BlockSpec(memory_space=pltpu.HBM), vmem),
         scratch_shapes=[
+            pltpu.VMEM(flat, f32),
             pltpu.VMEM(flat, f32),
             pltpu.VMEM(flat, jnp.int32),
             pltpu.VMEM((fields_n, cells, size_z), f32),
             pltpu.VMEM(flat, jnp.int32),
             pltpu.VMEM(stiffness.shape, f32),
             pltpu.VMEM(mass_matrix.shape, f32),
-            pltpu.VMEM((1, regions), f32),
+            pltpu.VMEM((regions,), f32),
             pltpu.VMEM((fields_n, (size_x + 1) * 2 * size_y, size_z), f32),
             pltpu.VMEM((fields_n, size_y, size_z), f32),
             pltpu.VMEM((fields_n, size_x, size_z), f32),
-            pltpu.VMEM((fields_n, size_z), f32),
+            pltpu.VMEM((pairs, 6, size_z), f32),
             pltpu.VMEM((fields_n, size_y, size_z), f32),
             pltpu.VMEM((fields_n, size_x, size_z), f32),
-            pltpu.VMEM((fields_n, size_z), f32),
+            pltpu.VMEM((pairs, 6, size_z), f32),
             pltpu.VMEM((2, 4, 2, size_x, size_z), f32),
             pltpu.VMEM((2, 8, 2, size_y, size_z), f32),
             pltpu.VMEM(((size_x + 4) * 3 * size_y, size_z), f32),
@@ -509,8 +526,9 @@
             pltpu.VMEM((ny, 8, size_z), f32),
             pltpu.VMEM((TRIALS // ny, size_z), f32),
             dma((7,)),
-            dma((3,)),
-            dma((3,)),
+            dma,
+            dma((pairs, 3)),
+            dma((pairs, 3)),
             dma((2, 8)),
             dma((2, 8)),
             dma((ny,)),
@@ -521,7 +539,7 @@
             dma((ny,)),
         ],
         compiler_params=pltpu.CompilerParams(
-            collective_id=0, has_side_effects=True, vmem_limit_bytes=48 * 1024 * 1024
+            collective_id=0, has_side_effects=True, vmem_limit_bytes=64 * 1024 * 1024
         ),
         name="sensitivity_update",
     )(
@@ -531,9 +549,14 @@
         supports.reshape(flat),
         stiffness,
         mass_matrix,
-        volume_fraction.reshape(1, regions),
+        volume_fraction,
     )
-    return tuple(out.reshape(design.shape) for out in outs)
+    negated = negated.reshape(design.shape)
+    trial = design * jnp.sqrt(jnp.maximum(negated, 0.0)) * inverse_root[None]
+    low = jnp.maximum(design - MOVE_LIMIT, 0.0)
+    high = jnp.minimum(design + MOVE_LIMIT, 1.0)
+    design_next = jnp.where(passive == 1, 1.0, jnp.minimum(high, jnp.maximum(low, trial)))
+    return -negated, design_next
 
 
 def solution(mesh):

time: 36.4 us -> 31.4 us (0.86)
  local copies, waits for them, and re-layouts: 6.7 us -> 0.01 us
  other arithmetic: 0 us -> 2.08 us
    unnamed x16 -> x2, local copies, waits for them, and re-layouts: 6.7 us -> 0.01 us
    select_n x0 -> x1, other arithmetic: none -> 1.46 us  [shards(): jnp.where(passive == 1, 1.0, jnp.minimum(high, jnp.maximum(low, trial)))]
    neg x0 -> x1, other arithmetic: none -> 0.62 us  [shards(): return (-negated, design_next)]
where the time goes in v3:
time: 31.4 us; the launch traced here: 31.1 us
  Pallas kernels  28.4 us (90%)
  other arithmetic  2.08 us (7%)
  between operations  0.65 us (2%)
    pallas_call x1, Pallas kernels, shards(): pl.pallas_call(functools.partial(kernel, nx, ny, size_x, size_y, size_z,...  28.4 us
    select_n x1, other arithmetic, shards(): jnp.where(passive == 1, 1.0, jnp.minimum(high, jnp.maximum(low, trial)))  1.46 us

profile of v3, /device:TPU:0, one launch (start us, length us, event | category | flops | bytes accessed | tf_op | source)
XLA Modules:
  0.0 31.1 jit_solution(2566571404101788417)
XLA Ops:
  0.6 28.4 %sensitivity_update.1 = (f32[64,128]{1,0:T(8,128)}, f32[8,128]{1,0:T(8,128)}) custom-call(f32[64,128]{1,0:T(8,128)} %bitcast.17, s32[64,128]{1,0:T(8,128)} %bitcast.18, f32[24,64,128]{2,1,0:T(8,128)} %bitcast.16, s32[64,128]{1,0:T(8,128)} %bitcast.19, f32[24,24]{1,0:T(8,128)} %stiffness_hbm.1, f32[24,24]{1,0:T(8,128)} %mass_hbm.1, f32[64]{0:T(128)} %fraction_hbm.1), custom_call_target="tpu_custom_call" | custom-call | tf_op jit(solution)/shard_map/sensitivity_update/pallas_call | solution.py:493
  29.0 0.0 copy-start
  29.1 1.5 %fusion.3 = f32[8,8,128]{2,1,0:T(8,128)} fusion(f32[8,8,128]{2,1,0:T(8,128)} %param.7, f32[64,128]{1,0:T(8,128)} %get-tuple-element.4, s32[8,8,128]{2,1,0:T(8,128)} %param.8, f32[8,128]{1,0:T(8,128)} %get-tuple-element.5), kind=kLoop, calls=%fused_computation.4 | loop fusion | flops 90112 | bytes 135168 | tf_op jit(solution)/shard_map/jit(_where)/select_n | solution.py:558
  30.5 0.0 copy-done
  30.5 0.6 %negate_bitcast_fusion = f32[8,8,128]{2,1,0:T(8,128)} fusion(f32[64,128]{1,0:T(8,128)S(1)} %copy-done), kind=kLoop, calls=%fused_computation.5 | loop fusion | flops 8192 | bytes 65536 | tf_op jit(solution)/shard_map/neg | solution.py:559
Async XLA Ops:
  29.0 1.5 %copy-start = (f32[64,128]{1,0:T(8,128)S(1)}, f32[64,128]{1,0:T(8,128)}, u32[]{:S(2)}) copy-start(f32[64,128]{1,0:T(8,128)} %get-tuple-element.4) | copy-start | bytes 98308

commit v4 on v3

--- a/solution.py
+++ b/solution.py
@@ -79,7 +79,7 @@
     design_hbm, passive_hbm, basis_hbm, supports_hbm, stiffness_hbm, mass_hbm, fraction_hbm,
     benefit_hbm, chosen_out,
     benefit, design, passive, basis, supports, stiffness, mass_matrix, fraction,
-    fields, send_x, send_y, send_c, recv_x, recv_y, recv_c,
+    fields, send_x, send_y, recv_x, recv_y,
     edge_send, edge_recv, wide, scaled, weights_hi, weights_lo, weight_sum, physical, energy,
     share_send, share_recv, gather_x, gather_y, leaf_table,
     load_sem, out_sem,
@@ -121,10 +121,10 @@
     free = 1.0 - supports[...].astype(jnp.float32)
     send_x[...] = basis[:, 0:size_y, :] * free[0:size_y][None]
     free_y = 1.0 - supports[pl.ds(0, size_x, stride=size_y), :].astype(jnp.float32)
+    send_y[...] = jnp.zeros(send_y.shape, jnp.float32)
     for f in range(6 * pairs):
         rows = basis[f, pl.ds(0, size_x, stride=size_y), :] * free_y
-        send_y[f] = rows
-        send_c[f // 6, pl.ds(f % 6, 1), :] = rows[0:1]
+        send_y[f // 6, pl.ds(f % 6, size_x, stride=8), :] = rows
 
     def pack_edges(source, which):
         for x in range(2):
@@ -199,29 +199,47 @@
     pack_edges(design, 0)
 
     grid_x, grid_y = nx * size_x, ny * size_y
-    wide_n, narrow_n = 24 * size_y, 24
+    wide_n, narrow_n, depth = 24 * size_y, 24, 16 * size_y
+    own_n = 12 * size_y
     bits_y = size_y.bit_length() - 1
-    row = lax.broadcasted_iota(jnp.int32, (wide_n, narrow_n), 0)
-    col = lax.broadcasted_iota(jnp.int32, (wide_n, narrow_n), 1)
-    expand = (lax.shift_right_logical(row, bits_y) == col).astype(jnp.float32).astype(jnp.bfloat16)
-    row_t = lax.broadcasted_iota(jnp.int32, (narrow_n, wide_n), 0)
-    col_t = lax.broadcasted_iota(jnp.int32, (narrow_n, wide_n), 1)
-    expand_t = (lax.shift_right_logical(col_t, bits_y) == row_t).astype(jnp.float32).astype(jnp.bfloat16)
-    same = (
-        lax.broadcasted_iota(jnp.int32, (wide_n, wide_n), 0) & (size_y - 1)
-        == lax.broadcasted_iota(jnp.int32, (wide_n, wide_n), 1) & (size_y - 1)
-    )
+
+    def spread_rows(shape, row_dim):
+        at = lax.broadcasted_iota(jnp.int32, shape, row_dim)
+        return lax.shift_right_logical(at, bits_y) == lax.broadcasted_iota(jnp.int32, shape, 1 - row_dim)
+
+    expand = spread_rows((wide_n, narrow_n), 0).astype(jnp.float32).astype(jnp.bfloat16)
+    col = lax.broadcasted_iota(jnp.int32, (narrow_n, depth), 1)
+    tile_of = lax.shift_right_logical(col, bits_y)
+    beyond = col >= own_n
+    corner = jnp.where(beyond, tile_of - 12, lax.shift_right_logical(tile_of * 11, 5))
+    component = jnp.where(beyond, (col & (size_y - 1)) - 3, tile_of - 3 * corner)
+    usable = (component >= 0) & (component < 3)
+    source_row = 12 * lax.shift_right_logical(corner, 1) + 3 * (corner & 1) + component
+    at_row = lax.broadcasted_iota(jnp.int32, (narrow_n, depth), 0)
+    gather = [
+        (usable & (at_row == source_row + 6 * b)).astype(jnp.float32).astype(jnp.bfloat16)
+        for b in range(2)
+    ]
+    at_y = lax.broadcasted_iota(jnp.int32, (wide_n, depth), 0) & (size_y - 1)
+    at_col = lax.broadcasted_iota(jnp.int32, (wide_n, depth), 1)
+    col_y = at_col & (size_y - 1)
+    own = at_col < own_n
+    keep = [
+        own & (col_y == at_y),
+        (own & (col_y == at_y + 1)) | (jnp.logical_not(own) & (at_y == size_y - 1)),
+    ]
 
     def spread_matrix(piece):
         tall = jnp.dot(expand, piece, preferred_element_type=jnp.float32).astype(jnp.bfloat16)
-        full = jnp.dot(tall, expand_t, preferred_element_type=jnp.float32)
-        return jnp.where(same, full, 0.0).astype(jnp.bfloat16)
+        full = [jnp.dot(tall, g, preferred_element_type=jnp.float32) for g in gather]
+        return jnp.where(keep[0], full[0], jnp.where(keep[1], full[1], 0.0)).astype(jnp.bfloat16)
 
     for k, matrix in enumerate((stiffness, mass_matrix)):
         value = matrix[...]
         high = value.astype(jnp.bfloat16)
         low = (value - high.astype(jnp.float32)).astype(jnp.bfloat16)
-        weights_hi[pl.ds(k * wide_n, wide_n), :] = spread_matrix(high)
+        spread_high = spread_matrix(high)
+        weights_hi[pl.ds(k * wide_n, wide_n), :] = jnp.concatenate([spread_high, spread_high], axis=1)
         weights_lo[pl.ds(k * wide_n, wide_n), :] = spread_matrix(low)
 
     band = size_z // regions
@@ -256,29 +274,36 @@
     pl.semaphore_wait(barrier, (nx - 1) + (ny - 1) + corners)
 
     design_copies = edge_copies(0)
-    edge_start(design_copies)
     basis_steps = ((-1, 0), (0, -1), (-1, -1))
     def basis_copies(pair):
         rows = pl.ds(pair * 6, 6)
+        ends = (
+            (send_x.at[rows], recv_x.at[rows]),
+            (send_y.at[pair], recv_y.at[pair, pl.ds(0, 8 * size_x)]),
+            (send_y.at[pair, pl.ds(0, 8)], recv_y.at[pair, pl.ds(8 * size_x, 8)]),
+        )
         return [
             pltpu.make_async_remote_copy(
-                src_ref=src.at[rows] if k < 2 else src.at[pair],
-                dst_ref=dst.at[rows] if k < 2 else dst.at[pair],
+                src_ref=src,
+                dst_ref=dst,
                 send_sem=basis_send_sem.at[pair, k],
                 recv_sem=basis_recv_sem.at[pair, k],
                 device_id=(ix + dx, iy + dy),
                 device_id_type=MESH,
             )
-            for k, ((dx, dy), src, dst) in enumerate(
-                zip(basis_steps, (send_x, send_y, send_c), (recv_x, recv_y, recv_c))
-            )
+            for k, ((dx, dy), (src, dst)) in enumerate(zip(basis_steps, ends))
         ]
 
-    for pair in range(pairs):
+    def basis_start(pair):
         for (dx, dy), copy in zip(basis_steps, basis_copies(pair)):
             @pl.when(there(dx, dy))
             def _(copy=copy):
                 copy.start()
+
+    basis_start(0)
+    edge_start(design_copies)
+    for pair in range(1, pairs):
+        basis_start(pair)
 
     for x in range(size_x):
         fields[:, x * pitch : x * pitch + size_y, :] = (
@@ -304,9 +329,13 @@
 
     energy[...] = jnp.zeros((2 * cells, size_z), jnp.float32)
 
+    order = [(a, b, d, c) for a in range(2) for b in range(2) for d in range(2) for c in range(3)]
+
     def pair_step(pair, carry):
         rows = pl.ds(pair * 6, 6)
-        buffers = (recv_x.at[rows], recv_y.at[rows], recv_c.at[pair])
+        buffers = (
+            recv_x.at[rows], recv_y.at[pair, pl.ds(0, 8 * size_x)], recv_y.at[pair, pl.ds(8 * size_x, 8)]
+        )
         for (dx, dy), copy, buffer in zip(basis_steps, basis_copies(pair), buffers):
             @pl.when(there(-dx, -dy))
             def _(copy=copy):
@@ -317,46 +346,49 @@
                 buffer[...] = jnp.zeros(buffer.shape, jnp.float32)
 
         fields[rows, size_x * pitch : size_x * pitch + size_y, :] = recv_x[rows]
-        for k in range(6):
-            f = pair * 6 + k
-            fields[f, pl.ds(size_y, size_x, stride=pitch), :] = recv_y[f]
-            fields[f, pl.ds(size_x * pitch + size_y, 1), :] = recv_c[pair, pl.ds(k, 1), :]
-
-        def corner_tiles(member):
-            tiles = {}
+        for k in range(3):
+            fields[pair * 6 + k, pl.ds(size_y, size_x + 1, stride=pitch), :] = (
+                recv_y[pair, pl.ds(k, size_x + 1, stride=8), :]
+            )
+
+        state, adjoint = {}, {}
+        for x in range(size_x + 1):
+            border = recv_y[pair, 8 * x : 8 * x + 8, :]
+            adjoint[3, x, 0], adjoint[3, x, 1] = border, z_shift(border, 1)
             for c in range(3):
-                f = pair * 6 + member * 3 + c
-                for x in range(size_x + 1):
-                    for b in range(2):
-                        tile = fields[f, x * pitch + b : x * pitch + b + size_y, :]
-                        tiles[c, x, b, 0] = tile
-                        tiles[c, x, b, 1] = z_shift(tile, 1)
-            return tiles
-
-        order = [(a, b, d, c) for a in range(2) for b in range(2) for d in range(2) for c in range(3)]
-        adjoint = corner_tiles(1)
-        operand = jnp.concatenate(
-            [
-                jnp.concatenate([adjoint[c, x + a, b, d] for x in range(size_x)], axis=1)
-                for a, b, d, c in order
-            ],
-            axis=0,
-        )
-        high = operand.astype(jnp.bfloat16)
-        low = (operand - high.astype(jnp.float32)).astype(jnp.bfloat16)
-        product = (
-            jnp.dot(weights_hi[...], high, preferred_element_type=jnp.float32)
-            + jnp.dot(weights_hi[...], low, preferred_element_type=jnp.float32)
-            + jnp.dot(weights_lo[...], high, preferred_element_type=jnp.float32)
-        )
-        state = corner_tiles(0)
-        for x in range(size_x):
-            for k in range(2):
-                total = energy[pl.ds((k * size_x + x) * size_y, size_y), :]
-                for r, (a, b, d, c) in enumerate(order):
-                    at = k * wide_n + r * size_y
-                    total = total + state[c, x + a, b, d] * product[at : at + size_y, x * size_z : (x + 1) * size_z]
-                energy[pl.ds((k * size_x + x) * size_y, size_y), :] = total
+                tile = fields[pair * 6 + 3 + c, x * pitch : x * pitch + size_y, :]
+                adjoint[c, x, 0], adjoint[c, x, 1] = tile, z_shift(tile, 1)
+                for b in range(2):
+                    tile = fields[pair * 6 + c, x * pitch + b : x * pitch + b + size_y, :]
+                    state[c, x, b, 0], state[c, x, b, 1] = tile, z_shift(tile, 1)
+
+        for first in range(0, size_x, 2):
+            planes = range(first, min(first + 2, size_x))
+            operand = jnp.concatenate(
+                [
+                    jnp.concatenate([adjoint[c, x + a, d] for x in planes], axis=1)
+                    for a, d, c in (
+                        [(a, d, c) for a in range(2) for d in range(2) for c in range(3)]
+                        + [(a, d, 3) for a in range(2) for d in range(2)]
+                    )
+                ],
+                axis=0,
+            )
+            high = operand.astype(jnp.bfloat16)
+            low = (operand - high.astype(jnp.float32)).astype(jnp.bfloat16)
+            product = jnp.dot(
+                weights_hi[...], jnp.concatenate([high, low], axis=0), preferred_element_type=jnp.float32
+            ) + jnp.dot(weights_lo[...], high, preferred_element_type=jnp.float32)
+            for at_x, x in enumerate(planes):
+                for k in range(2):
+                    total = energy[pl.ds((k * size_x + x) * size_y, size_y), :]
+                    for r, (a, b, d, c) in enumerate(order):
+                        at = k * wide_n + r * size_y
+                        total = total + (
+                            state[c, x + a, b, d]
+                            * product[at : at + size_y, at_x * size_z : (at_x + 1) * size_z]
+                        )
+                    energy[pl.ds((k * size_x + x) * size_y, size_y), :] = total
         return carry
 
     lax.fori_loop(0, pairs, pair_step, 0)
@@ -478,6 +510,15 @@
                 copy.wait_send()
     for copy in pending:
         copy.wait_send()
+
+
+def closing_kernel(negated, inverse_root, design, passive, sensitivity, design_next):
+    benefit, value = negated[...], design[...]
+    sensitivity[...] = -benefit
+    trial = value * jnp.sqrt(jnp.maximum(benefit, 0.0)) * inverse_root[0:1, :]
+    low = jnp.maximum(value - MOVE_LIMIT, 0.0)
+    high = jnp.minimum(value + MOVE_LIMIT, 1.0)
+    design_next[...] = jnp.where(passive[...] == 1, 1.0, jnp.minimum(high, jnp.maximum(low, trial)))
 
 
 def shards(nx, ny, design, passive, basis_pairs, supports, stiffness, mass_matrix, volume_fraction):
@@ -506,17 +547,15 @@
             pltpu.VMEM((regions,), f32),
             pltpu.VMEM((fields_n, (size_x + 1) * 2 * size_y, size_z), f32),
             pltpu.VMEM((fields_n, size_y, size_z), f32),
-            pltpu.VMEM((fields_n, size_x, size_z), f32),
-            pltpu.VMEM((pairs, 6, size_z), f32),
+            pltpu.VMEM((pairs, 8 * size_x, size_z), f32),
             pltpu.VMEM((fields_n, size_y, size_z), f32),
-            pltpu.VMEM((fields_n, size_x, size_z), f32),
-            pltpu.VMEM((pairs, 6, size_z), f32),
+            pltpu.VMEM((pairs, 8 * (size_x + 1), size_z), f32),
             pltpu.VMEM((2, 4, 2, size_x, size_z), f32),
             pltpu.VMEM((2, 8, 2, size_y, size_z), f32),
             pltpu.VMEM(((size_x + 4) * 3 * size_y, size_z), f32),
             pltpu.VMEM(flat, f32),
-            pltpu.VMEM((48 * size_y, 24 * size_y), bf16),
-            pltpu.VMEM((48 * size_y, 24 * size_y), bf16),
+            pltpu.VMEM((48 * size_y, 32 * size_y), bf16),
+            pltpu.VMEM((48 * size_y, 16 * size_y), bf16),
             pltpu.VMEM(flat, f32),
             pltpu.VMEM(flat, f32),
             pltpu.VMEM((2 * cells, size_z), f32),
@@ -551,12 +590,15 @@
         mass_matrix,
         volume_fraction,
     )
-    negated = negated.reshape(design.shape)
-    trial = design * jnp.sqrt(jnp.maximum(negated, 0.0)) * inverse_root[None]
-    low = jnp.maximum(design - MOVE_LIMIT, 0.0)
-    high = jnp.minimum(design + MOVE_LIMIT, 1.0)
-    design_next = jnp.where(passive == 1, 1.0, jnp.minimum(high, jnp.maximum(low, trial)))
-    return -negated, design_next
+    sensitivity, design_next = pl.pallas_call(
+        closing_kernel,
+        out_shape=(jax.ShapeDtypeStruct(flat, f32), jax.ShapeDtypeStruct(flat, f32)),
+        in_specs=[vmem] * 4,
+        out_specs=(vmem, vmem),
+        compiler_params=pltpu.CompilerParams(vmem_limit_bytes=64 * 1024 * 1024),
+        name="design_update",
+    )(negated, inverse_root, design.reshape(flat), passive.reshape(flat))
+    return sensitivity.reshape(design.shape), design_next.reshape(design.shape)
 
 
 def solution(mesh):

time: 31.4 us -> 30.2 us (0.962)
  other arithmetic: 2.08 us -> 0 us
  Pallas kernels: 28.4 us -> 29.4 us
    select_n x1 -> x0, other arithmetic: 1.46 us -> none  [shards(): jnp.where(passive == 1, 1.0, jnp.minimum(high, jnp.maximum(low, trial)))]
    pallas_call x0 -> x1, Pallas kernels: none -> 1.44 us  [shards(): pl.pallas_call(closing_kernel, out_shape=(jax.ShapeDtypeStruct(flat, f32)...]
    neg x1 -> x0, other arithmetic: 0.62 us -> none  [shards(): return (-negated, design_next)]
    pallas_call x1, Pallas kernels: 28.4 us -> 27.9 us  [shards(): pl.pallas_call(functools.partial(kernel, nx, ny, size_x, size_y, size_z,...]
where the time goes in v4:
time: 30.2 us; the launch traced here: 30 us
  Pallas kernels  29.4 us (97%)
  between operations  0.64 us (2%)
    pallas_call x1, Pallas kernels, shards(): pl.pallas_call(functools.partial(kernel, nx, ny, size_x, size_y, size_z,...  27.9 us
    pallas_call x1, Pallas kernels, shards(): pl.pallas_call(closing_kernel, out_shape=(jax.ShapeDtypeStruct(flat, f32)...  1.44 us

profile of v4, /device:TPU:0, one launch (start us, length us, event | category | flops | bytes accessed | tf_op | source)
XLA Modules:
  0.0 30.0 jit_solution(5450015644287141232)
XLA Ops:
  0.6 27.9 %sensitivity_update.1 = (f32[64,128]{1,0:T(8,128)}, f32[8,128]{1,0:T(8,128)}) custom-call(f32[64,128]{1,0:T(8,128)} %bitcast.7, s32[64,128]{1,0:T(8,128)} %bitcast.9, f32[24,64,128]{2,1,0:T(8,128)} %bitcast.6, s32[64,128]{1,0:T(8,128)} %bitcast.11, f32[24,24]{1,0:T(8,128)} %stiffness_hbm.1, f32[24,24]{1,0:T(8,128)} %mass_hbm.1, f32[64]{0:T(128)} %fraction_hbm.1), custom_call_target="tpu_custom_call" | custom-call | tf_op jit(solution)/shard_map/sensitivity_update/pallas_call | solution.py:534
  28.6 1.4 %design_update.1 = (f32[64,128]{1,0:T(8,128)}, f32[64,128]{1,0:T(8,128)}) custom-call(f32[64,128]{1,0:T(8,128)} %get-tuple-element.6.negated, f32[8,128]{1,0:T(8,128)} %get-tuple-element.7.inverse_root, f32[64,128]{1,0:T(8,128)} %bitcast.8, s32[64,128]{1,0:T(8,128)} %bitcast.10), custom_call_target="tpu_custom_call" | custom-call | tf_op jit(solution)/shard_map/design_update/pallas_call | solution.py:593

commit v5 on v4

--- a/solution.py
+++ b/solution.py
@@ -80,7 +80,7 @@
     benefit_hbm, chosen_out,
     benefit, design, passive, basis, supports, stiffness, mass_matrix, fraction,
     fields, send_x, send_y, recv_x, recv_y,
-    edge_send, edge_recv, wide, scaled, weights_hi, weights_lo, weight_sum, physical, energy,
+    edge_send, edge_recv, wide, scaled, weights_hi, weights_lo, border_hi, border_lo, weight_sum, physical, energy,
     share_send, share_recv, gather_x, gather_y, leaf_table,
     load_sem, out_sem,
     basis_send_sem, basis_recv_sem, halo_send_sem, halo_recv_sem,
@@ -95,6 +95,9 @@
             (ix + dx >= 0) & (ix + dx < nx) & (iy + dy >= 0) & (iy + dy < ny)
         )
 
+    edge_recv[...] = jnp.zeros(edge_recv.shape, jnp.float32)
+    recv_x[...] = jnp.zeros(recv_x.shape, jnp.float32)
+    recv_y[...] = jnp.zeros(recv_y.shape, jnp.float32)
     barrier = pltpu.get_barrier_semaphore()
     for step in range(1, ny):
         pl.semaphore_signal(barrier, inc=1, device_id=(ix, lax.rem(iy + step, ny)), device_id_type=MESH)
@@ -115,13 +118,13 @@
     ]
     for load in loads:
         load.start()
-    for load in loads:
+    send_y[...] = jnp.zeros(send_y.shape, jnp.float32)
+    for load in loads[:2]:
         load.wait()
 
     free = 1.0 - supports[...].astype(jnp.float32)
     send_x[...] = basis[:, 0:size_y, :] * free[0:size_y][None]
     free_y = 1.0 - supports[pl.ds(0, size_x, stride=size_y), :].astype(jnp.float32)
-    send_y[...] = jnp.zeros(send_y.shape, jnp.float32)
     for f in range(6 * pairs):
         rows = basis[f, pl.ds(0, size_x, stride=size_y), :] * free_y
         send_y[f // 6, pl.ds(f % 6, size_x, stride=8), :] = rows
@@ -151,29 +154,14 @@
             ))
         return copies
 
-    def edge_start(copies):
-        for (dx, dy), copy in zip(AROUND, copies):
+    def edge_each(copies, act):
+        for slot, (dx, dy) in enumerate(AROUND):
             @pl.when(there(dx, dy))
-            def _(copy=copy):
-                copy.start()
-
-    def edge_receive(copies, which):
-        for slot, (dx, dy) in enumerate(AROUND):
-            copy = copies[opposite(slot)]
-
-            @pl.when(there(dx, dy))
-            def _(copy=copy):
-                copy.wait_recv()
-
-            @pl.when(jnp.logical_not(there(dx, dy)))
             def _(slot=slot):
-                edge_recv[which, slot] = jnp.zeros((2, size_y, size_z), jnp.float32)
-
-    def edge_finish(copies):
-        for (dx, dy), copy in zip(AROUND, copies):
-            @pl.when(there(dx, dy))
-            def _(copy=copy):
-                copy.wait_send()
+                act(copies, slot)
+
+    def edge_receive(copies):
+        edge_each(copies, lambda c, slot: c[opposite(slot)].wait_recv())
 
     span = 3 * size_y
 
@@ -196,11 +184,44 @@
     def wide_rows(plane, oy):
         return wide[pl.ds(plane * span + size_y + oy, size_y), :]
 
+    loads[2].wait()
     pack_edges(design, 0)
 
+    pl.semaphore_wait(barrier, (nx - 1) + (ny - 1) + corners)
+
+    design_copies = edge_copies(0)
+    basis_copies = {
+        slot: pltpu.make_async_remote_copy(
+            src_ref=src,
+            dst_ref=dst,
+            send_sem=basis_send_sem.at[k],
+            recv_sem=basis_recv_sem.at[k],
+            device_id=(ix + AROUND[slot][0], iy + AROUND[slot][1]),
+            device_id_type=MESH,
+        )
+        for k, (slot, src, dst) in enumerate((
+            (0, send_x, recv_x),
+            (2, send_y, recv_y.at[:, pl.ds(0, 8 * size_x)]),
+            (4, send_y.at[:, pl.ds(0, 8)], recv_y.at[:, pl.ds(8 * size_x, 8)]),
+        ))
+    }
+
+    def leave(copies, slot):
+        if slot in basis_copies:
+            basis_copies[slot].start()
+        copies[slot].start()
+
+    def left(copies, slot):
+        if slot in basis_copies:
+            basis_copies[slot].wait_send()
+        copies[slot].wait_send()
+
+    edge_each(design_copies, leave)
+    for load in loads[3:]:
+        load.wait()
+
     grid_x, grid_y = nx * size_x, ny * size_y
-    wide_n, narrow_n, depth = 24 * size_y, 24, 16 * size_y
-    own_n = 12 * size_y
+    wide_n, narrow_n, depth = 24 * size_y, 24, 12 * size_y
     bits_y = size_y.bit_length() - 1
 
     def spread_rows(shape, row_dim):
@@ -210,37 +231,38 @@
     expand = spread_rows((wide_n, narrow_n), 0).astype(jnp.float32).astype(jnp.bfloat16)
     col = lax.broadcasted_iota(jnp.int32, (narrow_n, depth), 1)
     tile_of = lax.shift_right_logical(col, bits_y)
-    beyond = col >= own_n
-    corner = jnp.where(beyond, tile_of - 12, lax.shift_right_logical(tile_of * 11, 5))
-    component = jnp.where(beyond, (col & (size_y - 1)) - 3, tile_of - 3 * corner)
-    usable = (component >= 0) & (component < 3)
+    corner = lax.shift_right_logical(tile_of * 11, 5)
+    component = tile_of - 3 * corner
     source_row = 12 * lax.shift_right_logical(corner, 1) + 3 * (corner & 1) + component
     at_row = lax.broadcasted_iota(jnp.int32, (narrow_n, depth), 0)
     gather = [
-        (usable & (at_row == source_row + 6 * b)).astype(jnp.float32).astype(jnp.bfloat16)
+        (at_row == source_row + 6 * b).astype(jnp.float32).astype(jnp.bfloat16)
         for b in range(2)
     ]
     at_y = lax.broadcasted_iota(jnp.int32, (wide_n, depth), 0) & (size_y - 1)
-    at_col = lax.broadcasted_iota(jnp.int32, (wide_n, depth), 1)
-    col_y = at_col & (size_y - 1)
-    own = at_col < own_n
-    keep = [
-        own & (col_y == at_y),
-        (own & (col_y == at_y + 1)) | (jnp.logical_not(own) & (at_y == size_y - 1)),
-    ]
+    col_y = lax.broadcasted_iota(jnp.int32, (wide_n, depth), 1) & (size_y - 1)
+    keep = [col_y == at_y, col_y == at_y + 1]
+    expand_t = spread_rows((narrow_n, wide_n), 1).astype(jnp.float32).astype(jnp.bfloat16)
+    same = (
+        lax.broadcasted_iota(jnp.int32, (wide_n, wide_n), 0) & (size_y - 1)
+    ) == (lax.broadcasted_iota(jnp.int32, (wide_n, wide_n), 1) & (size_y - 1))
 
     def spread_matrix(piece):
         tall = jnp.dot(expand, piece, preferred_element_type=jnp.float32).astype(jnp.bfloat16)
         full = [jnp.dot(tall, g, preferred_element_type=jnp.float32) for g in gather]
-        return jnp.where(keep[0], full[0], jnp.where(keep[1], full[1], 0.0)).astype(jnp.bfloat16)
+        banded = jnp.where(keep[0], full[0], jnp.where(keep[1], full[1], 0.0))
+        plain = jnp.where(same, jnp.dot(tall, expand_t, preferred_element_type=jnp.float32), 0.0)
+        return banded.astype(jnp.bfloat16), plain.astype(jnp.bfloat16)
 
     for k, matrix in enumerate((stiffness, mass_matrix)):
         value = matrix[...]
         high = value.astype(jnp.bfloat16)
         low = (value - high.astype(jnp.float32)).astype(jnp.bfloat16)
-        spread_high = spread_matrix(high)
-        weights_hi[pl.ds(k * wide_n, wide_n), :] = jnp.concatenate([spread_high, spread_high], axis=1)
-        weights_lo[pl.ds(k * wide_n, wide_n), :] = spread_matrix(low)
+        at = pl.ds(k * wide_n, wide_n)
+        banded, plain = spread_matrix(high)
+        weights_hi[at, :] = jnp.concatenate([banded, banded], axis=1)
+        border_hi[at, :] = plain
+        weights_lo[at, :], border_lo[at, :] = spread_matrix(low)
 
     band = size_z // regions
     width, group_rows = size_z // ny, TRIALS // ny
@@ -271,40 +293,8 @@
             line = jnp.where(lane8[0:1] // width == g, INVERSE_LEAVES[j], line)
         leaf_table[pl.ds(r, 1), :] = line
 
-    pl.semaphore_wait(barrier, (nx - 1) + (ny - 1) + corners)
-
-    design_copies = edge_copies(0)
-    basis_steps = ((-1, 0), (0, -1), (-1, -1))
-    def basis_copies(pair):
-        rows = pl.ds(pair * 6, 6)
-        ends = (
-            (send_x.at[rows], recv_x.at[rows]),
-            (send_y.at[pair], recv_y.at[pair, pl.ds(0, 8 * size_x)]),
-            (send_y.at[pair, pl.ds(0, 8)], recv_y.at[pair, pl.ds(8 * size_x, 8)]),
-        )
-        return [
-            pltpu.make_async_remote_copy(
-                src_ref=src,
-                dst_ref=dst,
-                send_sem=basis_send_sem.at[pair, k],
-                recv_sem=basis_recv_sem.at[pair, k],
-                device_id=(ix + dx, iy + dy),
-                device_id_type=MESH,
-            )
-            for k, ((dx, dy), (src, dst)) in enumerate(zip(basis_steps, ends))
-        ]
-
-    def basis_start(pair):
-        for (dx, dy), copy in zip(basis_steps, basis_copies(pair)):
-            @pl.when(there(dx, dy))
-            def _(copy=copy):
-                copy.start()
-
-    basis_start(0)
-    edge_start(design_copies)
-    for pair in range(1, pairs):
-        basis_start(pair)
-
+    for x in range(size_x + 1):
+        fields[:, x * pitch + size_y : (x + 1) * pitch, :] = jnp.zeros((6 * pairs, size_y, size_z), jnp.float32)
     for x in range(size_x):
         fields[:, x * pitch : x * pitch + size_y, :] = (
             basis[:, x * size_y : (x + 1) * size_y, :] * free[x * size_y : (x + 1) * size_y][None]
@@ -321,77 +311,119 @@
     for x, tile in enumerate(stencil(inside, size_x)):
         weight_sum[pl.ds(x * size_y, size_y), :] = tile
 
-    edge_receive(design_copies, 0)
+    energy[...] = jnp.zeros((2 * cells, size_z), jnp.float32)
+    order = [(a, b, d, c) for a in range(2) for b in range(2) for d in range(2) for c in range(3)]
+
+    def beside(tiles):
+        return tiles[0] if len(tiles) == 1 else jnp.concatenate(tiles, axis=1)
+
+    def split(operand):
+        high = operand.astype(jnp.bfloat16)
+        return high, (operand - high.astype(jnp.float32)).astype(jnp.bfloat16)
+
+    def contract(product, states):
+        return [
+            [
+                functools.reduce(
+                    lambda p, q: p + q,
+                    [
+                        state[key] * product[
+                            k * wide_n + r * size_y : k * wide_n + (r + 1) * size_y,
+                            n * size_z : (n + 1) * size_z,
+                        ]
+                        for r, key in enumerate(order)
+                    ],
+                )
+                for k in range(2)
+            ]
+            for n, state in enumerate(states)
+        ]
+
+    def name_of(pair):
+        return pair if isinstance(pair, int) else -1
+
+    def own_columns(columns):
+        adjoint, state = {}, {}
+        for pair, x in columns:
+            for c in range(3):
+                for at_x in (x, x + 1):
+                    key = (name_of(pair), at_x, c)
+                    if key in adjoint:
+                        continue
+                    tile = fields[pair * 6 + 3 + c, at_x * pitch : at_x * pitch + size_y, :]
+                    adjoint[key] = (tile, z_shift(tile, 1))
+                    for b in range(2):
+                        tile = fields[pair * 6 + c, at_x * pitch + b : at_x * pitch + b + size_y, :]
+                        state[key + (b,)] = (tile, z_shift(tile, 1))
+        high, low = split(jnp.concatenate(
+            [
+                beside([adjoint[name_of(pair), x + a, c][d] for pair, x in columns])
+                for a in range(2) for d in range(2) for c in range(3)
+            ],
+            axis=0,
+        ))
+        product = jnp.dot(
+            weights_hi[...], jnp.concatenate([high, low], axis=0), preferred_element_type=jnp.float32
+        ) + jnp.dot(weights_lo[...], high, preferred_element_type=jnp.float32)
+        states = [
+            {(a, b, d, c): state[name_of(pair), x + a, c, b][d] for a, b, d, c in order} for pair, x in columns
+        ]
+        for (pair, x), parts in zip(columns, contract(product, states)):
+            for k, part in enumerate(parts):
+                at = pl.ds((k * size_x + x) * size_y, size_y)
+                energy[at, :] = energy[at, :] + part
+
+    def pair_step(pair, carry):
+        for first in range(0, size_x - 1, 2):
+            own_columns([(pair, x) for x in range(first, min(first + 2, size_x - 1))])
+        return carry
+
+    lax.fori_loop(0, pairs, pair_step, 0)
+
+    edge_receive(design_copies)
     assemble(design, 0)
     for x, tile in enumerate(stencil(wide_rows, size_x)):
         at = pl.ds(x * size_y, size_y)
         physical[at, :] = jnp.where(passive[at, :] == 1, 1.0, tile / weight_sum[at, :])
 
-    energy[...] = jnp.zeros((2 * cells, size_z), jnp.float32)
-
-    order = [(a, b, d, c) for a in range(2) for b in range(2) for d in range(2) for c in range(3)]
-
-    def pair_step(pair, carry):
-        rows = pl.ds(pair * 6, 6)
-        buffers = (
-            recv_x.at[rows], recv_y.at[pair, pl.ds(0, 8 * size_x)], recv_y.at[pair, pl.ds(8 * size_x, 8)]
+    for slot in basis_copies:
+        dx, dy = AROUND[slot]
+
+        @pl.when(there(-dx, -dy))
+        def _(slot=slot):
+            basis_copies[slot].wait_recv()
+
+    fields[:, size_x * pitch : size_x * pitch + size_y, :] = recv_x[...]
+    for first in range(0, pairs, 2):
+        own_columns([(pair, size_x - 1) for pair in range(first, min(first + 2, pairs))])
+
+    def border_tiles(pair, member):
+        tiles = {}
+        for c in range(3):
+            f, k = pair * 6 + member * 3 + c, member * 3 + c
+            for a in range(2):
+                for b in range(2):
+                    if b == 0:
+                        tile = fields[f, pl.ds(a * pitch + size_y - 1, size_x, stride=pitch), :]
+                    else:
+                        tile = recv_y[pair, pl.ds(8 * a + k, size_x, stride=8), :]
+                    tiles[a, b, 0, c], tiles[a, b, 1, c] = tile, z_shift(tile, 1)
+        return tiles
+
+    border = [None, None]
+    for first in range(0, pairs, 2):
+        group_pairs = range(first, min(first + 2, pairs))
+        adjoints = [border_tiles(pair, 1) for pair in group_pairs]
+        high, low = split(jnp.concatenate([beside([t[key] for t in adjoints]) for key in order], axis=0))
+        product = (
+            jnp.dot(border_hi[...], high, preferred_element_type=jnp.float32)
+            + jnp.dot(border_hi[...], low, preferred_element_type=jnp.float32)
+            + jnp.dot(border_lo[...], high, preferred_element_type=jnp.float32)
         )
-        for (dx, dy), copy, buffer in zip(basis_steps, basis_copies(pair), buffers):
-            @pl.when(there(-dx, -dy))
-            def _(copy=copy):
-                copy.wait_recv()
-
-            @pl.when(jnp.logical_not(there(-dx, -dy)))
-            def _(buffer=buffer):
-                buffer[...] = jnp.zeros(buffer.shape, jnp.float32)
-
-        fields[rows, size_x * pitch : size_x * pitch + size_y, :] = recv_x[rows]
-        for k in range(3):
-            fields[pair * 6 + k, pl.ds(size_y, size_x + 1, stride=pitch), :] = (
-                recv_y[pair, pl.ds(k, size_x + 1, stride=8), :]
-            )
-
-        state, adjoint = {}, {}
-        for x in range(size_x + 1):
-            border = recv_y[pair, 8 * x : 8 * x + 8, :]
-            adjoint[3, x, 0], adjoint[3, x, 1] = border, z_shift(border, 1)
-            for c in range(3):
-                tile = fields[pair * 6 + 3 + c, x * pitch : x * pitch + size_y, :]
-                adjoint[c, x, 0], adjoint[c, x, 1] = tile, z_shift(tile, 1)
-                for b in range(2):
-                    tile = fields[pair * 6 + c, x * pitch + b : x * pitch + b + size_y, :]
-                    state[c, x, b, 0], state[c, x, b, 1] = tile, z_shift(tile, 1)
-
-        for first in range(0, size_x, 2):
-            planes = range(first, min(first + 2, size_x))
-            operand = jnp.concatenate(
-                [
-                    jnp.concatenate([adjoint[c, x + a, d] for x in planes], axis=1)
-                    for a, d, c in (
-                        [(a, d, c) for a in range(2) for d in range(2) for c in range(3)]
-                        + [(a, d, 3) for a in range(2) for d in range(2)]
-                    )
-                ],
-                axis=0,
-            )
-            high = operand.astype(jnp.bfloat16)
-            low = (operand - high.astype(jnp.float32)).astype(jnp.bfloat16)
-            product = jnp.dot(
-                weights_hi[...], jnp.concatenate([high, low], axis=0), preferred_element_type=jnp.float32
-            ) + jnp.dot(weights_lo[...], high, preferred_element_type=jnp.float32)
-            for at_x, x in enumerate(planes):
-                for k in range(2):
-                    total = energy[pl.ds((k * size_x + x) * size_y, size_y), :]
-                    for r, (a, b, d, c) in enumerate(order):
-                        at = k * wide_n + r * size_y
-                        total = total + (
-                            state[c, x + a, b, d]
-                            * product[at : at + size_y, at_x * size_z : (at_x + 1) * size_z]
-                        )
-                    energy[pl.ds((k * size_x + x) * size_y, size_y), :] = total
-        return carry
-
-    lax.fori_loop(0, pairs, pair_step, 0)
+        for parts in contract(product, [border_tiles(pair, 0) for pair in group_pairs]):
+            border = [p if e is None else e + p for e, p in zip(border, parts)]
+    for k in range(2):
+        energy[pl.ds(k * cells + size_y - 1, size_x, stride=size_y), :] = border[k]
 
     solid = passive[...] == 1
     density = physical[...]
@@ -403,8 +435,9 @@
 
     pack_edges(scaled, 1)
     scaled_copies = edge_copies(1)
-    edge_start(scaled_copies)
-    edge_receive(scaled_copies, 1)
+    edge_each(scaled_copies, lambda c, slot: c[slot].start())
+    edge_each(design_copies, left)
+    edge_receive(scaled_copies)
     assemble(scaled, 1)
     for x, tile in enumerate(stencil(wide_rows, size_x)):
         benefit[pl.ds(x * size_y, size_y), :] = -tile
@@ -501,13 +534,7 @@
     chosen_out[...] = multiplier
     benefit_out.wait()
 
-    edge_finish(design_copies)
-    edge_finish(scaled_copies)
-    for pair in range(pairs):
-        for (dx, dy), copy in zip(basis_steps, basis_copies(pair)):
-            @pl.when(there(dx, dy))
-            def _(copy=copy):
-                copy.wait_send()
+    edge_each(scaled_copies, lambda c, slot: c[slot].wait_send())
     for copy in pending:
         copy.wait_send()
 
@@ -554,8 +581,10 @@
             pltpu.VMEM((2, 8, 2, size_y, size_z), f32),
             pltpu.VMEM(((size_x + 4) * 3 * size_y, size_z), f32),
             pltpu.VMEM(flat, f32),
-            pltpu.VMEM((48 * size_y, 32 * size_y), bf16),
-            pltpu.VMEM((48 * size_y, 16 * size_y), bf16),
+            pltpu.VMEM((48 * size_y, 24 * size_y), bf16),
+            pltpu.VMEM((48 * size_y, 12 * size_y), bf16),
+            pltpu.VMEM((48 * size_y, 24 * size_y), bf16),
+            pltpu.VMEM((48 * size_y, 24 * size_y), bf16),
             pltpu.VMEM(flat, f32),
             pltpu.VMEM(flat, f32),
             pltpu.VMEM((2 * cells, size_z), f32),
@@ -566,8 +595,8 @@
             pltpu.VMEM((TRIALS // ny, size_z), f32),
             dma((7,)),
             dma,
-            dma((pairs, 3)),
-            dma((pairs, 3)),
+            dma((3,)),
+            dma((3,)),
             dma((2, 8)),
             dma((2, 8)),
             dma((ny,)),

time: 30.2 us -> 29.7 us (0.983)
  Pallas kernels: 29.4 us -> 28.8 us
    pallas_call x1, Pallas kernels: 27.9 us -> 27.4 us  [shards(): pl.pallas_call(functools.partial(kernel, nx, ny, size_x, size_y, size_z,...]
where the time goes in v5:
time: 29.7 us; the launch traced here: 29.5 us
  Pallas kernels  28.8 us (97%)
  between operations  0.64 us (2%)
    pallas_call x1, Pallas kernels, shards(): pl.pallas_call(functools.partial(kernel, nx, ny, size_x, size_y, size_z,...  27.4 us
    pallas_call x1, Pallas kernels, shards(): pl.pallas_call(closing_kernel, out_shape=(jax.ShapeDtypeStruct(flat, f32)...  1.44 us

profile of v5, /device:TPU:0, one launch (start us, length us, event | category | flops | bytes accessed | tf_op | source)
XLA Modules:
  0.0 29.5 jit_solution(8357303295503264)
XLA Ops:
  0.6 27.4 %sensitivity_update.1 = (f32[64,128]{1,0:T(8,128)}, f32[8,128]{1,0:T(8,128)}) custom-call(f32[64,128]{1,0:T(8,128)} %bitcast.7, s32[64,128]{1,0:T(8,128)} %bitcast.9, f32[24,64,128]{2,1,0:T(8,128)} %bitcast.6, s32[64,128]{1,0:T(8,128)} %bitcast.11, f32[24,24]{1,0:T(8,128)} %stiffness_hbm.1, f32[24,24]{1,0:T(8,128)} %mass_hbm.1, f32[64]{0:T(128)} %fraction_hbm.1), custom_call_target="tpu_custom_call" | custom-call | tf_op jit(solution)/shard_map/sensitivity_update/pallas_call | solution.py:561
  28.0 1.4 %design_update.1 = (f32[64,128]{1,0:T(8,128)}, f32[64,128]{1,0:T(8,128)}) custom-call(f32[64,128]{1,0:T(8,128)} %get-tuple-element.6.negated, f32[8,128]{1,0:T(8,128)} %get-tuple-element.7.inverse_root, f32[64,128]{1,0:T(8,128)} %bitcast.8, s32[64,128]{1,0:T(8,128)} %bitcast.10), custom_call_target="tpu_custom_call" | custom-call | tf_op jit(solution)/shard_map/design_update/pallas_call | solution.py:622

commit v6 on v5

--- a/solution.py
+++ b/solution.py
@@ -14,6 +14,7 @@
 MOVE_LIMIT = 0.2
 BISECT = 6
 TRIALS = 2**BISECT
+CHUNK = 4
 MESH = pl.DeviceIdType.MESH
 AROUND = ((-1, 0), (1, 0), (0, -1), (0, 1), (-1, -1), (-1, 1), (1, -1), (1, 1))
 
@@ -47,25 +48,28 @@
     return jnp.where(keep, moved, 0.0)
 
 
+def fold_plane(tiles):
+    folded_y = (tiles[2], tiles[1] + tiles[3], tiles[0] + tiles[4])
+    parts = [[], [], []]
+    for cy, tile in enumerate(folded_y):
+        folded_z = (
+            tile,
+            z_shift(tile, 1) + z_shift(tile, -1),
+            z_shift(tile, 2) + z_shift(tile, -2),
+        )
+        for cz, entry in enumerate(folded_z):
+            for cx in range(3):
+                weight = 3.0 - math.sqrt(cx * cx + cy * cy + cz * cz)
+                if weight > 0.0:
+                    parts[cx].append(weight * entry)
+    return [functools.reduce(lambda a, b: a + b, part) for part in parts]
+
+
 def stencil(rows_at, size_x):
-    spread = [[None] * (size_x + 4) for _ in range(3)]
-    for plane in range(size_x + 4):
-        tiles = [rows_at(plane, oy) for oy in range(-2, 3)]
-        folded_y = (tiles[2], tiles[1] + tiles[3], tiles[0] + tiles[4])
-        parts = [[], [], []]
-        for cy, tile in enumerate(folded_y):
-            folded_z = (
-                tile,
-                z_shift(tile, 1) + z_shift(tile, -1),
-                z_shift(tile, 2) + z_shift(tile, -2),
-            )
-            for cz, entry in enumerate(folded_z):
-                for cx in range(3):
-                    weight = 3.0 - math.sqrt(cx * cx + cy * cy + cz * cz)
-                    if weight > 0.0:
-                        parts[cx].append(weight * entry)
-        for cx in range(3):
-            spread[cx][plane] = functools.reduce(lambda a, b: a + b, parts[cx])
+    planes = [
+        fold_plane([rows_at(plane, oy) for oy in range(-2, 3)]) for plane in range(size_x + 4)
+    ]
+    spread = [[plane[cx] for plane in planes] for cx in range(3)]
     return [
         spread[0][i + 2]
         + (spread[1][i + 1] + spread[1][i + 3])
@@ -228,7 +232,6 @@
         at = lax.broadcasted_iota(jnp.int32, shape, row_dim)
         return lax.shift_right_logical(at, bits_y) == lax.broadcasted_iota(jnp.int32, shape, 1 - row_dim)
 
-    expand = spread_rows((wide_n, narrow_n), 0).astype(jnp.float32).astype(jnp.bfloat16)
     col = lax.broadcasted_iota(jnp.int32, (narrow_n, depth), 1)
     tile_of = lax.shift_right_logical(col, bits_y)
     corner = lax.shift_right_logical(tile_of * 11, 5)
@@ -242,27 +245,182 @@
     at_y = lax.broadcasted_iota(jnp.int32, (wide_n, depth), 0) & (size_y - 1)
     col_y = lax.broadcasted_iota(jnp.int32, (wide_n, depth), 1) & (size_y - 1)
     keep = [col_y == at_y, col_y == at_y + 1]
-    expand_t = spread_rows((narrow_n, wide_n), 1).astype(jnp.float32).astype(jnp.bfloat16)
     same = (
         lax.broadcasted_iota(jnp.int32, (wide_n, wide_n), 0) & (size_y - 1)
     ) == (lax.broadcasted_iota(jnp.int32, (wide_n, wide_n), 1) & (size_y - 1))
 
-    def spread_matrix(piece):
-        tall = jnp.dot(expand, piece, preferred_element_type=jnp.float32).astype(jnp.bfloat16)
-        full = [jnp.dot(tall, g, preferred_element_type=jnp.float32) for g in gather]
-        banded = jnp.where(keep[0], full[0], jnp.where(keep[1], full[1], 0.0))
-        plain = jnp.where(same, jnp.dot(tall, expand_t, preferred_element_type=jnp.float32), 0.0)
-        return banded.astype(jnp.bfloat16), plain.astype(jnp.bfloat16)
-
-    for k, matrix in enumerate((stiffness, mass_matrix)):
+    pieces = []
+    for matrix in (stiffness, mass_matrix):
         value = matrix[...]
-        high = value.astype(jnp.bfloat16)
-        low = (value - high.astype(jnp.float32)).astype(jnp.bfloat16)
+        high = value.astype(jnp.bfloat16).astype(jnp.float32)
+        pieces += [high, value - high]
+    pieces = jnp.concatenate(pieces, axis=0).astype(jnp.bfloat16)
+    expand = spread_rows((4 * wide_n, 4 * narrow_n), 0).astype(jnp.float32).astype(jnp.bfloat16)
+    tall = jnp.dot(expand, pieces, preferred_element_type=jnp.float32).astype(jnp.bfloat16)
+    plain_gather = spread_rows((narrow_n, wide_n), 1).astype(jnp.float32).astype(jnp.bfloat16)
+    banded_full = [jnp.dot(tall, g, preferred_element_type=jnp.float32) for g in gather]
+    plain_full = jnp.dot(tall, plain_gather, preferred_element_type=jnp.float32)
+    for k in range(2):
         at = pl.ds(k * wide_n, wide_n)
-        banded, plain = spread_matrix(high)
-        weights_hi[at, :] = jnp.concatenate([banded, banded], axis=1)
-        border_hi[at, :] = plain
-        weights_lo[at, :], border_lo[at, :] = spread_matrix(low)
+        for half in range(2):
+            rows = slice((2 * k + half) * wide_n, (2 * k + half + 1) * wide_n)
+            banded = jnp.where(
+                keep[0], banded_full[0][rows], jnp.where(keep[1], banded_full[1][rows], 0.0)
+            ).astype(jnp.bfloat16)
+            plain = jnp.where(same, plain_full[rows], 0.0).astype(jnp.bfloat16)
+            if half == 0:
+                weights_hi[at, :] = jnp.concatenate([banded, banded], axis=1)
+                border_hi[at, :] = plain
+            else:
+                weights_lo[at, :] = banded
+                border_lo[at, :] = plain
+
+    for x in range(size_x + 1):
+        fields[:, x * pitch + size_y : (x + 1) * pitch, :] = jnp.zeros((6 * pairs, size_y, size_z), jnp.float32)
+    for x in range(size_x):
+        fields[:, x * pitch : x * pitch + size_y, :] = (
+            basis[:, x * size_y : (x + 1) * size_y, :] * free[x * size_y : (x + 1) * size_y][None]
+        )
+
+    row_y = lax.broadcasted_iota(jnp.int32, (size_y, size_z), 0)
+
+    def inside_y(oy):
+        at_y = row_y + (iy * size_y + oy)
+        return jnp.where((at_y >= 0) & (at_y < grid_y), 1.0, 0.0)
+
+    def inside_x(plane):
+        at_x = jnp.full((size_y, size_z), ix * size_x + plane - 2, jnp.int32)
+        return jnp.where((at_x >= 0) & (at_x < grid_x), 1.0, 0.0)
+
+    share_of = fold_plane([inside_y(oy) for oy in range(-2, 3)])
+    flags = [inside_x(plane) for plane in range(size_x + 4)]
+    for x in range(size_x):
+        weight_sum[pl.ds(x * size_y, size_y), :] = (
+            share_of[0]
+            + (flags[x + 1] + flags[x + 3]) * share_of[1]
+            + (flags[x] + flags[x + 4]) * share_of[2]
+        )
+
+    energy[...] = jnp.zeros((2 * cells, size_z), jnp.float32)
+    order = [(a, b, d, c) for a in range(2) for b in range(2) for d in range(2) for c in range(3)]
+
+    def beside(tiles):
+        return tiles[0] if len(tiles) == 1 else jnp.concatenate(tiles, axis=1)
+
+    def split(operand):
+        high = operand.astype(jnp.bfloat16)
+        return high, (operand - high.astype(jnp.float32)).astype(jnp.bfloat16)
+
+    def contract(product, states):
+        return [
+            [
+                functools.reduce(
+                    lambda p, q: p + q,
+                    [
+                        state[key] * product[
+                            k * wide_n + r * size_y : k * wide_n + (r + 1) * size_y,
+                            n * size_z : (n + 1) * size_z,
+                        ]
+                        for r, key in enumerate(order)
+                    ],
+                )
+                for k in range(2)
+            ]
+            for n, state in enumerate(states)
+        ]
+
+    def own_columns(columns):
+        adjoint, state = {}, {}
+        for pair, x in columns:
+            for c in range(3):
+                for at_x in (x, x + 1):
+                    key = (pair, at_x, c)
+                    if key in adjoint:
+                        continue
+                    tile = fields[pair * 6 + 3 + c, at_x * pitch : at_x * pitch + size_y, :]
+                    adjoint[key] = (tile, z_shift(tile, 1))
+                    for b in range(2):
+                        tile = fields[pair * 6 + c, at_x * pitch + b : at_x * pitch + b + size_y, :]
+                        state[key + (b,)] = (tile, z_shift(tile, 1))
+        high, low = split(jnp.concatenate(
+            [
+                beside([adjoint[pair, x + a, c][d] for pair, x in columns])
+                for a in range(2) for d in range(2) for c in range(3)
+            ],
+            axis=0,
+        ))
+        product = jnp.dot(
+            weights_hi[...], jnp.concatenate([high, low], axis=0), preferred_element_type=jnp.float32
+        ) + jnp.dot(weights_lo[...], high, preferred_element_type=jnp.float32)
+        states = [
+            {(a, b, d, c): state[pair, x + a, c, b][d] for a, b, d, c in order} for pair, x in columns
+        ]
+        for (pair, x), parts in zip(columns, contract(product, states)):
+            for k, part in enumerate(parts):
+                at = pl.ds((k * size_x + x) * size_y, size_y)
+                energy[at, :] = energy[at, :] + part
+
+    for pair in range(pairs):
+        for first in range(0, size_x - 1, CHUNK):
+            own_columns([(pair, x) for x in range(first, min(first + CHUNK, size_x - 1))])
+
+    edge_receive(design_copies)
+    assemble(design, 0)
+    for x, tile in enumerate(stencil(wide_rows, size_x)):
+        at = pl.ds(x * size_y, size_y)
+        physical[at, :] = jnp.where(passive[at, :] == 1, 1.0, tile / weight_sum[at, :])
+
+    for slot in basis_copies:
+        dx, dy = AROUND[slot]
+
+        @pl.when(there(-dx, -dy))
+        def _(slot=slot):
+            basis_copies[slot].wait_recv()
+
+    fields[:, size_x * pitch : size_x * pitch + size_y, :] = recv_x[...]
+    for first in range(0, pairs, CHUNK):
+        own_columns([(pair, size_x - 1) for pair in range(first, min(first + CHUNK, pairs))])
+
+    def border_tiles(pair, member):
+        tiles = {}
+        for c in range(3):
+            f, k = pair * 6 + member * 3 + c, member * 3 + c
+            for a in range(2):
+                for b in range(2):
+                    if b == 0:
+                        tile = fields[f, pl.ds(a * pitch + size_y - 1, size_x, stride=pitch), :]
+                    else:
+                        tile = recv_y[pair, pl.ds(8 * a + k, size_x, stride=8), :]
+                    tiles[a, b, 0, c], tiles[a, b, 1, c] = tile, z_shift(tile, 1)
+        return tiles
+
+    border = [None, None]
+    for first in range(0, pairs, CHUNK):
+        group_pairs = range(first, min(first + CHUNK, pairs))
+        adjoints = [border_tiles(pair, 1) for pair in group_pairs]
+        high, low = split(jnp.concatenate([beside([t[key] for t in adjoints]) for key in order], axis=0))
+        product = (
+            jnp.dot(border_hi[...], high, preferred_element_type=jnp.float32)
+            + jnp.dot(border_hi[...], low, preferred_element_type=jnp.float32)
+            + jnp.dot(border_lo[...], high, preferred_element_type=jnp.float32)
+        )
+        for parts in contract(product, [border_tiles(pair, 0) for pair in group_pairs]):
+            border = [p if e is None else e + p for e, p in zip(border, parts)]
+    for k in range(2):
+        energy[pl.ds(k * cells + size_y - 1, size_x, stride=size_y), :] = border[k]
+
+    solid = passive[...] == 1
+    density = physical[...]
+    raw = -(
+        PENALTY_SCALE * density * density * energy[0:cells, :]
+        - OMEGA_SQUARED * energy[cells : 2 * cells, :]
+    )
+    scaled[...] = jnp.where(solid, 0.0, raw) / weight_sum[...]
+
+    pack_edges(scaled, 1)
+    scaled_copies = edge_copies(1)
+    edge_each(scaled_copies, lambda c, slot: c[slot].start())
+    edge_each(design_copies, left)
 
     band = size_z // regions
     width, group_rows = size_z // ny, TRIALS // ny
@@ -293,150 +451,6 @@
             line = jnp.where(lane8[0:1] // width == g, INVERSE_LEAVES[j], line)
         leaf_table[pl.ds(r, 1), :] = line
 
-    for x in range(size_x + 1):
-        fields[:, x * pitch + size_y : (x + 1) * pitch, :] = jnp.zeros((6 * pairs, size_y, size_z), jnp.float32)
-    for x in range(size_x):
-        fields[:, x * pitch : x * pitch + size_y, :] = (
-            basis[:, x * size_y : (x + 1) * size_y, :] * free[x * size_y : (x + 1) * size_y][None]
-        )
-
-    row_y = lax.broadcasted_iota(jnp.int32, (size_y, size_z), 0)
-
-    def inside(plane, oy):
-        at_x = ix * size_x + plane - 2
-        at_y = row_y + (iy * size_y + oy)
-        ok = (at_y >= 0) & (at_y < grid_y) & (at_x >= 0) & (at_x < grid_x)
-        return jnp.where(ok, 1.0, 0.0)
-
-    for x, tile in enumerate(stencil(inside, size_x)):
-        weight_sum[pl.ds(x * size_y, size_y), :] = tile
-
-    energy[...] = jnp.zeros((2 * cells, size_z), jnp.float32)
-    order = [(a, b, d, c) for a in range(2) for b in range(2) for d in range(2) for c in range(3)]
-
-    def beside(tiles):
-        return tiles[0] if len(tiles) == 1 else jnp.concatenate(tiles, axis=1)
-
-    def split(operand):
-        high = operand.astype(jnp.bfloat16)
-        return high, (operand - high.astype(jnp.float32)).astype(jnp.bfloat16)
-
-    def contract(product, states):
-        return [
-            [
-                functools.reduce(
-                    lambda p, q: p + q,
-                    [
-                        state[key] * product[
-                            k * wide_n + r * size_y : k * wide_n + (r + 1) * size_y,
-                            n * size_z : (n + 1) * size_z,
-                        ]
-                        for r, key in enumerate(order)
-                    ],
-                )
-                for k in range(2)
-            ]
-            for n, state in enumerate(states)
-        ]
-
-    def name_of(pair):
-        return pair if isinstance(pair, int) else -1
-
-    def own_columns(columns):
-        adjoint, state = {}, {}
-        for pair, x in columns:
-            for c in range(3):
-                for at_x in (x, x + 1):
-                    key = (name_of(pair), at_x, c)
-                    if key in adjoint:
-                        continue
-                    tile = fields[pair * 6 + 3 + c, at_x * pitch : at_x * pitch + size_y, :]
-                    adjoint[key] = (tile, z_shift(tile, 1))
-                    for b in range(2):
-                        tile = fields[pair * 6 + c, at_x * pitch + b : at_x * pitch + b + size_y, :]
-                        state[key + (b,)] = (tile, z_shift(tile, 1))
-        high, low = split(jnp.concatenate(
-            [
-                beside([adjoint[name_of(pair), x + a, c][d] for pair, x in columns])
-                for a in range(2) for d in range(2) for c in range(3)
-            ],
-            axis=0,
-        ))
-        product = jnp.dot(
-            weights_hi[...], jnp.concatenate([high, low], axis=0), preferred_element_type=jnp.float32
-        ) + jnp.dot(weights_lo[...], high, preferred_element_type=jnp.float32)
-        states = [
-            {(a, b, d, c): state[name_of(pair), x + a, c, b][d] for a, b, d, c in order} for pair, x in columns
-        ]
-        for (pair, x), parts in zip(columns, contract(product, states)):
-            for k, part in enumerate(parts):
-                at = pl.ds((k * size_x + x) * size_y, size_y)
-                energy[at, :] = energy[at, :] + part
-
-    def pair_step(pair, carry):
-        for first in range(0, size_x - 1, 2):
-            own_columns([(pair, x) for x in range(first, min(first + 2, size_x - 1))])
-        return carry
-
-    lax.fori_loop(0, pairs, pair_step, 0)
-
-    edge_receive(design_copies)
-    assemble(design, 0)
-    for x, tile in enumerate(stencil(wide_rows, size_x)):
-        at = pl.ds(x * size_y, size_y)
-        physical[at, :] = jnp.where(passive[at, :] == 1, 1.0, tile / weight_sum[at, :])
-
-    for slot in basis_copies:
-        dx, dy = AROUND[slot]
-
-        @pl.when(there(-dx, -dy))
-        def _(slot=slot):
-            basis_copies[slot].wait_recv()
-
-    fields[:, size_x * pitch : size_x * pitch + size_y, :] = recv_x[...]
-    for first in range(0, pairs, 2):
-        own_columns([(pair, size_x - 1) for pair in range(first, min(first + 2, pairs))])
-
-    def border_tiles(pair, member):
-        tiles = {}
-        for c in range(3):
-            f, k = pair * 6 + member * 3 + c, member * 3 + c
-            for a in range(2):
-                for b in range(2):
-                    if b == 0:
-                        tile = fields[f, pl.ds(a * pitch + size_y - 1, size_x, stride=pitch), :]
-                    else:
-                        tile = recv_y[pair, pl.ds(8 * a + k, size_x, stride=8), :]
-                    tiles[a, b, 0, c], tiles[a, b, 1, c] = tile, z_shift(tile, 1)
-        return tiles
-
-    border = [None, None]
-    for first in range(0, pairs, 2):
-        group_pairs = range(first, min(first + 2, pairs))
-        adjoints = [border_tiles(pair, 1) for pair in group_pairs]
-        high, low = split(jnp.concatenate([beside([t[key] for t in adjoints]) for key in order], axis=0))
-        product = (
-            jnp.dot(border_hi[...], high, preferred_element_type=jnp.float32)
-            + jnp.dot(border_hi[...], low, preferred_element_type=jnp.float32)
-            + jnp.dot(border_lo[...], high, preferred_element_type=jnp.float32)
-        )
-        for parts in contract(product, [border_tiles(pair, 0) for pair in group_pairs]):
-            border = [p if e is None else e + p for e, p in zip(border, parts)]
-    for k in range(2):
-        energy[pl.ds(k * cells + size_y - 1, size_x, stride=size_y), :] = border[k]
-
-    solid = passive[...] == 1
-    density = physical[...]
-    raw = -(
-        PENALTY_SCALE * density * density * energy[0:cells, :]
-        - OMEGA_SQUARED * energy[cells : 2 * cells, :]
-    )
-    scaled[...] = jnp.where(solid, 0.0, raw) / weight_sum[...]
-
-    pack_edges(scaled, 1)
-    scaled_copies = edge_copies(1)
-    edge_each(scaled_copies, lambda c, slot: c[slot].start())
-    edge_each(design_copies, left)
     edge_receive(scaled_copies)
     assemble(scaled, 1)
     for x, tile in enumerate(stencil(wide_rows, size_x)):

time: 29.7 us -> 29.7 us (level)
  no operation moved by 1% of the time
where the time goes in v6:
time: 29.7 us; the launch traced here: 29.5 us
  Pallas kernels  28.9 us (97%)
  between operations  0.64 us (2%)
    pallas_call x1, Pallas kernels, shards(): pl.pallas_call(functools.partial(kernel, nx, ny, size_x, size_y, size_z,...  27.4 us
    pallas_call x1, Pallas kernels, shards(): pl.pallas_call(closing_kernel, out_shape=(jax.ShapeDtypeStruct(flat, f32)...  1.44 us

profile of v6, /device:TPU:0, one launch (start us, length us, event | category | flops | bytes accessed | tf_op | source)
XLA Modules:
  0.0 29.5 jit_solution(5704631548002317022)
XLA Ops:
  0.6 27.4 %sensitivity_update.1 = (f32[64,128]{1,0:T(8,128)}, f32[8,128]{1,0:T(8,128)}) custom-call(f32[64,128]{1,0:T(8,128)} %bitcast.7, s32[64,128]{1,0:T(8,128)} %bitcast.9, f32[24,64,128]{2,1,0:T(8,128)} %bitcast.6, s32[64,128]{1,0:T(8,128)} %bitcast.11, f32[24,24]{1,0:T(8,128)} %stiffness_hbm.1, f32[24,24]{1,0:T(8,128)} %mass_hbm.1, f32[64]{0:T(128)} %fraction_hbm.1), custom_call_target="tpu_custom_call" | custom-call | tf_op jit(solution)/shard_map/sensitivity_update/pallas_call | solution.py:575
  28.1 1.4 %design_update.1 = (f32[64,128]{1,0:T(8,128)}, f32[64,128]{1,0:T(8,128)}) custom-call(f32[64,128]{1,0:T(8,128)} %get-tuple-element.6.negated, f32[8,128]{1,0:T(8,128)} %get-tuple-element.7.inverse_root, f32[64,128]{1,0:T(8,128)} %bitcast.8, s32[64,128]{1,0:T(8,128)} %bitcast.10), custom_call_target="tpu_custom_call" | custom-call | tf_op jit(solution)/shard_map/design_update/pallas_call | solution.py:636

commit v7 on v6

--- a/solution.py
+++ b/solution.py
@@ -85,7 +85,7 @@
     benefit, design, passive, basis, supports, stiffness, mass_matrix, fraction,
     fields, send_x, send_y, recv_x, recv_y,
     edge_send, edge_recv, wide, scaled, weights_hi, weights_lo, border_hi, border_lo, weight_sum, physical, energy,
-    share_send, share_recv, gather_x, gather_y, leaf_table,
+    share_send, share_recv, gather_x, gather_y, leaf_table, middle_table, volume_table,
     load_sem, out_sem,
     basis_send_sem, basis_recv_sem, halo_send_sem, halo_recv_sem,
     share_send_sem, share_recv_sem, gx_send_sem, gx_recv_sem, gy_send_sem, gy_recv_sem,
@@ -191,36 +191,6 @@
     loads[2].wait()
     pack_edges(design, 0)
 
-    pl.semaphore_wait(barrier, (nx - 1) + (ny - 1) + corners)
-
-    design_copies = edge_copies(0)
-    basis_copies = {
-        slot: pltpu.make_async_remote_copy(
-            src_ref=src,
-            dst_ref=dst,
-            send_sem=basis_send_sem.at[k],
-            recv_sem=basis_recv_sem.at[k],
-            device_id=(ix + AROUND[slot][0], iy + AROUND[slot][1]),
-            device_id_type=MESH,
-        )
-        for k, (slot, src, dst) in enumerate((
-            (0, send_x, recv_x),
-            (2, send_y, recv_y.at[:, pl.ds(0, 8 * size_x)]),
-            (4, send_y.at[:, pl.ds(0, 8)], recv_y.at[:, pl.ds(8 * size_x, 8)]),
-        ))
-    }
-
-    def leave(copies, slot):
-        if slot in basis_copies:
-            basis_copies[slot].start()
-        copies[slot].start()
-
-    def left(copies, slot):
-        if slot in basis_copies:
-            basis_copies[slot].wait_send()
-        copies[slot].wait_send()
-
-    edge_each(design_copies, leave)
     for load in loads[3:]:
         load.wait()
 
@@ -301,6 +271,40 @@
             + (flags[x] + flags[x + 4]) * share_of[2]
         )
 
+    for j in range(TRIALS - 1):
+        middle_table[pl.ds(j, 1), :] = jnp.full((1, size_z), INVERSE_MIDDLES[j], jnp.float32)
+    middle_table[pl.ds(TRIALS - 1, 1), :] = jnp.zeros((1, size_z), jnp.float32)
+
+    pl.semaphore_wait(barrier, (nx - 1) + (ny - 1) + corners)
+
+    design_copies = edge_copies(0)
+    basis_copies = {
+        slot: pltpu.make_async_remote_copy(
+            src_ref=src,
+            dst_ref=dst,
+            send_sem=basis_send_sem.at[k],
+            recv_sem=basis_recv_sem.at[k],
+            device_id=(ix + AROUND[slot][0], iy + AROUND[slot][1]),
+            device_id_type=MESH,
+        )
+        for k, (slot, src, dst) in enumerate((
+            (0, send_x, recv_x),
+            (2, send_y, recv_y.at[:, pl.ds(0, 8 * size_x)]),
+            (4, send_y.at[:, pl.ds(0, 8)], recv_y.at[:, pl.ds(8 * size_x, 8)]),
+        ))
+    }
+
+    def leave(copies, slot):
+        if slot in basis_copies:
+            basis_copies[slot].start()
+        copies[slot].start()
+
+    def left(copies, slot):
+        if slot in basis_copies:
+            basis_copies[slot].wait_send()
+        copies[slot].wait_send()
+
+    edge_each(design_copies, leave)
     energy[...] = jnp.zeros((2 * cells, size_z), jnp.float32)
     order = [(a, b, d, c) for a in range(2) for b in range(2) for d in range(2) for c in range(3)]
 
@@ -329,12 +333,15 @@
             for n, state in enumerate(states)
         ]
 
+    def name_of(pair):
+        return pair if isinstance(pair, int) else -1
+
     def own_columns(columns):
         adjoint, state = {}, {}
         for pair, x in columns:
             for c in range(3):
                 for at_x in (x, x + 1):
-                    key = (pair, at_x, c)
+                    key = (name_of(pair), at_x, c)
                     if key in adjoint:
                         continue
                     tile = fields[pair * 6 + 3 + c, at_x * pitch : at_x * pitch + size_y, :]
@@ -344,7 +351,7 @@
                         state[key + (b,)] = (tile, z_shift(tile, 1))
         high, low = split(jnp.concatenate(
             [
-                beside([adjoint[pair, x + a, c][d] for pair, x in columns])
+                beside([adjoint[name_of(pair), x + a, c][d] for pair, x in columns])
                 for a in range(2) for d in range(2) for c in range(3)
             ],
             axis=0,
@@ -353,16 +360,19 @@
             weights_hi[...], jnp.concatenate([high, low], axis=0), preferred_element_type=jnp.float32
         ) + jnp.dot(weights_lo[...], high, preferred_element_type=jnp.float32)
         states = [
-            {(a, b, d, c): state[pair, x + a, c, b][d] for a, b, d, c in order} for pair, x in columns
+            {(a, b, d, c): state[name_of(pair), x + a, c, b][d] for a, b, d, c in order} for pair, x in columns
         ]
         for (pair, x), parts in zip(columns, contract(product, states)):
             for k, part in enumerate(parts):
                 at = pl.ds((k * size_x + x) * size_y, size_y)
                 energy[at, :] = energy[at, :] + part
 
-    for pair in range(pairs):
+    def pair_step(pair, carry):
         for first in range(0, size_x - 1, CHUNK):
             own_columns([(pair, x) for x in range(first, min(first + CHUNK, size_x - 1))])
+        return carry
+
+    lax.fori_loop(0, pairs, pair_step, 0)
 
     edge_receive(design_copies)
     assemble(design, 0)
@@ -467,17 +477,14 @@
         return jnp.minimum(ceiling, jnp.maximum(floor_value, gain * inverse_root))
 
     def total_over_x(j):
-        trial = candidate(INVERSE_MIDDLES[j])
+        trial = candidate(middle_table[pl.ds(j, 1), :])
         return functools.reduce(
             lambda p, q: p + q, [trial[x * size_y : (x + 1) * size_y] for x in range(size_x)]
         )
 
-    volumes = []
-    for first in range(0, TRIALS, 8):
-        tiles = [
-            total_over_x(j) if j < TRIALS - 1 else jnp.zeros((8, size_z), jnp.float32)
-            for j in range(first, first + 8)
-        ]
+    def trial_group(number, carry):
+        first = pl.multiple_of(number * 8, 8)
+        tiles = [total_over_x(first + j) for j in range(8)]
         reach = 4
         while reach:
             lower = (slot_row & reach) == 0
@@ -487,8 +494,12 @@
                 for p, q in zip(tiles[:reach], tiles[reach:])
             ]
             reach //= 2
-        volumes.append(tiles[0])
-    volumes = jnp.concatenate(volumes, axis=0)
+        unused = slot_row + first == TRIALS - 1
+        volume_table[pl.ds(first, 8), :] = jnp.where(unused, 0.0, tiles[0])
+        return carry
+
+    lax.fori_loop(0, TRIALS // 8, trial_group, 0)
+    volumes = volume_table[...]
 
     for q in range(ny):
         packed = jnp.zeros((group_rows, size_z), jnp.float32)
@@ -607,6 +618,8 @@
             pltpu.VMEM((nx, TRIALS // ny, size_z), f32),
             pltpu.VMEM((ny, 8, size_z), f32),
             pltpu.VMEM((TRIALS // ny, size_z), f32),
+            pltpu.VMEM((TRIALS, size_z), f32),
+            pltpu.VMEM((TRIALS, size_z), f32),
             dma((7,)),
             dma,
             dma((3,)),

time: 29.7 us -> 30.2 us (1.017)
  Pallas kernels: 28.9 us -> 29.3 us
    pallas_call x1, Pallas kernels: 27.4 us -> 27.9 us  [shards(): pl.pallas_call(functools.partial(kernel, nx, ny, size_x, size_y, size_z,...]
where the time goes in v7:
time: 30.2 us; the launch traced here: 30 us
  Pallas kernels  29.3 us (97%)
  between operations  0.64 us (2%)
    pallas_call x1, Pallas kernels, shards(): pl.pallas_call(functools.partial(kernel, nx, ny, size_x, size_y, size_z,...  27.9 us
    pallas_call x1, Pallas kernels, shards(): pl.pallas_call(closing_kernel, out_shape=(jax.ShapeDtypeStruct(flat, f32)...  1.44 us

profile of v7, /device:TPU:0, one launch (start us, length us, event | category | flops | bytes accessed | tf_op | source)
XLA Modules:
  0.0 30.0 jit_solution(11125711616174796215)
XLA Ops:
  0.6 27.9 %sensitivity_update.1 = (f32[64,128]{1,0:T(8,128)}, f32[8,128]{1,0:T(8,128)}) custom-call(f32[64,128]{1,0:T(8,128)} %bitcast.7, s32[64,128]{1,0:T(8,128)} %bitcast.9, f32[24,64,128]{2,1,0:T(8,128)} %bitcast.6, s32[64,128]{1,0:T(8,128)} %bitcast.11, f32[24,24]{1,0:T(8,128)} %stiffness_hbm.1, f32[24,24]{1,0:T(8,128)} %mass_hbm.1, f32[64]{0:T(128)} %fraction_hbm.1), custom_call_target="tpu_custom_call" | custom-call | tf_op jit(solution)/shard_map/sensitivity_update/pallas_call | solution.py:586
  28.5 1.4 %design_update.1 = (f32[64,128]{1,0:T(8,128)}, f32[64,128]{1,0:T(8,128)}) custom-call(f32[64,128]{1,0:T(8,128)} %get-tuple-element.6.negated, f32[8,128]{1,0:T(8,128)} %get-tuple-element.7.inverse_root, f32[64,128]{1,0:T(8,128)} %bitcast.8, s32[64,128]{1,0:T(8,128)} %bitcast.10), custom_call_target="tpu_custom_call" | custom-call | tf_op jit(solution)/shard_map/design_update/pallas_call | solution.py:649

commit v8 on v6

--- a/solution.py
+++ b/solution.py
@@ -424,7 +424,8 @@
 
     band = size_z // regions
     width, group_rows = size_z // ny, TRIALS // ny
-    lane = lax.broadcasted_iota(jnp.int32, (group_rows, size_z), 1)
+    part_rows = group_rows // band
+    lane = lax.broadcasted_iota(jnp.int32, (part_rows, size_z), 1)
     lane8 = lax.broadcasted_iota(jnp.int32, (8, size_z), 1)
     slot_row = lax.broadcasted_iota(jnp.int32, (8, size_z), 0)
     group = lane // width
@@ -444,11 +445,13 @@
     while reach < size_z:
         own_target = own_target + pltpu.roll(own_target, reach, 1)
         reach *= 2
-    for r in range(group_rows):
+    for r in range(part_rows):
         line = jnp.full((1, size_z), INVERSE_LEAVES[0], jnp.float32)
         for g in range(ny):
-            j = min(g * group_rows + r + 1, TRIALS - 1)
-            line = jnp.where(lane8[0:1] // width == g, INVERSE_LEAVES[j], line)
+            for place in range(band):
+                j = min(g * group_rows + place * part_rows + r + 1, TRIALS - 1)
+                here = (lane8[0:1] // width == g) & ((lane8[0:1] & (band - 1)) == place)
+                line = jnp.where(here, INVERSE_LEAVES[j], line)
         leaf_table[pl.ds(r, 1), :] = line
 
     edge_receive(scaled_copies)
@@ -490,10 +493,23 @@
         volumes.append(tiles[0])
     volumes = jnp.concatenate(volumes, axis=0)
 
+    reach = 1
+    lane_all = lax.broadcasted_iota(jnp.int32, volumes.shape, 1)
+    while reach < band:
+        volumes = volumes + jnp.where(
+            (lane_all & reach) == 0,
+            pltpu.roll(volumes, size_z - reach, 1),
+            pltpu.roll(volumes, reach, 1),
+        )
+        reach *= 2
+
     for q in range(ny):
-        packed = jnp.zeros((group_rows, size_z), jnp.float32)
+        packed = jnp.zeros((part_rows, size_z), jnp.float32)
         for g in range(ny):
-            part = volumes[g * group_rows : (g + 1) * group_rows]
+            part = volumes[g * group_rows : g * group_rows + part_rows]
+            for place in range(1, band):
+                first = g * group_rows + place * part_rows
+                part = jnp.where((lane & (band - 1)) == place, volumes[first : first + part_rows], part)
             turn = (width * (g - q)) % size_z
             if turn:
                 part = pltpu.roll(part, turn, 1)
@@ -526,16 +542,16 @@
     along(nx, ix, lambda at: (at, iy), lambda at: gather_x.at[ix], gather_x, gx_send_sem, gx_recv_sem)
     share = functools.reduce(lambda p, q: p + q, [gather_x[k] for k in range(nx)])
 
+    chosen = jnp.where(share > own_target[0:1], leaf_table[...], INVERSE_LEAVES[0])
+    chosen = jnp.min(chosen, axis=0, keepdims=True)
     reach = 1
     while reach < band:
-        share = share + jnp.where(
-            (lane // reach) % 2 == 0,
-            pltpu.roll(share, size_z - reach, 1),
-            pltpu.roll(share, reach, 1),
-        )
+        chosen = jnp.minimum(chosen, jnp.where(
+            (lane8[0:1] & reach) == 0,
+            pltpu.roll(chosen, size_z - reach, 1),
+            pltpu.roll(chosen, reach, 1),
+        ))
         reach *= 2
-    chosen = jnp.where(share > own_target[0:1], leaf_table[...], INVERSE_LEAVES[0])
-    chosen = jnp.min(chosen, axis=0, keepdims=True)
     reach = width
     while reach < size_z:
         chosen = jnp.minimum(chosen, pltpu.roll(chosen, reach, 1))
@@ -569,6 +585,7 @@
     cells = size_x * size_y
     fields_n = 6 * pairs
     flat = (cells, size_z)
+    share_rows = TRIALS // ny * regions // size_z
     vmem = pl.BlockSpec(memory_space=pltpu.VMEM)
     f32, bf16 = jnp.float32, jnp.bfloat16
     dma = pltpu.SemaphoreType.DMA
@@ -602,11 +619,11 @@
             pltpu.VMEM(flat, f32),
             pltpu.VMEM(flat, f32),
             pltpu.VMEM((2 * cells, size_z), f32),
-            pltpu.VMEM((ny, TRIALS // ny, size_z), f32),
-            pltpu.VMEM((ny, TRIALS // ny, size_z), f32),
-            pltpu.VMEM((nx, TRIALS // ny, size_z), f32),
+            pltpu.VMEM((ny, share_rows, size_z), f32),
+            pltpu.VMEM((ny, share_rows, size_z), f32),
+            pltpu.VMEM((nx, share_rows, size_z), f32),
             pltpu.VMEM((ny, 8, size_z), f32),
-            pltpu.VMEM((TRIALS // ny, size_z), f32),
+            pltpu.VMEM((share_rows, size_z), f32),
             dma((7,)),
             dma,
             dma((3,)),

time: 29.7 us -> 29.5 us (level)
  Pallas kernels: 28.9 us -> 28.6 us
where the time goes in v8:
time: 29.5 us; the launch traced here: 29.2 us
  Pallas kernels  28.6 us (97%)
  between operations  0.64 us (2%)
    pallas_call x1, Pallas kernels, shards(): pl.pallas_call(functools.partial(kernel, nx, ny, size_x, size_y, size_z,...  27.2 us
    pallas_call x1, Pallas kernels, shards(): pl.pallas_call(closing_kernel, out_shape=(jax.ShapeDtypeStruct(flat, f32)...  1.44 us

profile of v8, /device:TPU:0, one launch (start us, length us, event | category | flops | bytes accessed | tf_op | source)
XLA Modules:
  0.0 29.2 jit_solution(722403343413184386)
XLA Ops:
  0.6 27.2 %sensitivity_update.1 = (f32[64,128]{1,0:T(8,128)}, f32[8,128]{1,0:T(8,128)}) custom-call(f32[64,128]{1,0:T(8,128)} %bitcast.7, s32[64,128]{1,0:T(8,128)} %bitcast.9, f32[24,64,128]{2,1,0:T(8,128)} %bitcast.6, s32[64,128]{1,0:T(8,128)} %bitcast.11, f32[24,24]{1,0:T(8,128)} %stiffness_hbm.1, f32[24,24]{1,0:T(8,128)} %mass_hbm.1, f32[64]{0:T(128)} %fraction_hbm.1), custom_call_target="tpu_custom_call" | custom-call | tf_op jit(solution)/shard_map/sensitivity_update/pallas_call | solution.py:592
  27.8 1.4 %design_update.1 = (f32[64,128]{1,0:T(8,128)}, f32[64,128]{1,0:T(8,128)}) custom-call(f32[64,128]{1,0:T(8,128)} %get-tuple-element.6.negated, f32[8,128]{1,0:T(8,128)} %get-tuple-element.7.inverse_root, f32[64,128]{1,0:T(8,128)} %bitcast.8, s32[64,128]{1,0:T(8,128)} %bitcast.10), custom_call_target="tpu_custom_call" | custom-call | tf_op jit(solution)/shard_map/design_update/pallas_call | solution.py:653
